TPU v7x, 128 devices: a whole 4x4x4 slice. The times are simulated.
128 devices in a mesh: grid: 32 (over x, y, core), basis: 4 (over z).
Axes of the slice: x: 4, y: 4, z: 4, core: 2. Of those that a mesh axis runs over, the one named last changes fastest.
Arguments:
- density: bfloat16 [64, 12, 128, 1408], P('grid', None, 'basis'), may hold values from -0.0078125 to 0.0078125
- basis_vals: bfloat16 [256, 256, 768], P('grid'), may hold values from -6 to 6
- kernel: float32 [256, 256], P('grid'), may hold values from -0.12 to -0.02
- starts: int32 [256], P('grid'), may hold values from 0 to 58, as said below
- counts: int32 [256], P('grid'), may hold values from 32 to 256
- pair_mask: int32 [64, 11], replicated, may hold values 0 or 1
Outputs:
- fock_response: float32 [64, 12, 128, 1408], P('grid', None, 'basis')
Inputs may be any that keep to these rules, and one draw needn't show every extreme that they name: `starts`: the batches held by grid index g (batches g * 8 to g * 8 + 7) start between max(g * 2 - 5, 0) and min(g * 2 + 1, 58), both ends taken on every grid index.
All inputs are finite; a program needn't handle non-finite values.
Results may differ from a plain program's by a relative error of at most 0.0003.
Values may be sent and summed in bfloat16 or wider, within the bound.
A program may use at most 256 MiB of HBM per device.

v0:
```python
import jax
import jax.numpy as jnp
from jax import lax
from jax.sharding import PartitionSpec as P

BLOCK = 128
PERTS = 12
WINDOW = 6
POINTS = 256
REACH = 5
BAND = 11


def passed_along(block, axis, distance):
    devices = range(lax.axis_size(axis))
    route = [(i - distance, i) for i in devices if i - distance in devices]
    return lax.ppermute(block, axis, route)


def own_columns(phi_vals, row_first, row_share):
    reshaped = phi_vals.reshape(phi_vals.shape[0], WINDOW, BLOCK)
    own_cut = lax.dynamic_slice_in_dim(reshaped, row_first, row_share, 2)
    return own_cut.reshape(phi_vals.shape[0], WINDOW * row_share)


def window_slab(dens_slab, start_local):
    row_share = dens_slab.shape[2]
    slab_rows = lax.dynamic_slice_in_dim(dens_slab, start_local, WINDOW, 0)
    column_parts = []
    for offset in range(WINDOW):
        lead_block = REACH - offset
        column_parts.append(
            slab_rows[offset, :, :, lead_block * BLOCK : (lead_block + WINDOW) * BLOCK]
        )
    stacked = jnp.stack(column_parts, axis=1)
    return stacked.reshape(PERTS, WINDOW * row_share, WINDOW * BLOCK)


def partial_densities(dens_slab, phi_all, local_starts, row_first, row_share):

    def one_batch(batch_data):
        phi_vals, start_local = batch_data
        win_dens = window_slab(dens_slab, start_local)
        own_vals = own_columns(phi_vals, row_first, row_share)
        mixed_vals = jnp.einsum(
            "pc,krc->kpr", phi_vals, win_dens, preferred_element_type=jnp.float32
        )
        return jnp.sum(own_vals.astype(jnp.float32)[None] * mixed_vals, axis=2)

    return lax.map(one_batch, (phi_all, local_starts))


def accumulate(wide_rows, phi_all, local_starts, potential, row_first, row_share):
    running = jnp.zeros((wide_rows, PERTS, row_share, BAND * BLOCK), jnp.float32)

    def add_batch(batch_no, running):
        phi_vals = phi_all[batch_no]
        own_vals = own_columns(phi_vals, row_first, row_share)
        weighted = potential[batch_no][:, :, None] * own_vals[None].astype(jnp.float32)
        fock_win = jnp.einsum(
            "kpr,pc->krc",
            weighted,
            phi_vals.astype(jnp.float32),
            precision=lax.Precision.HIGHEST,
            preferred_element_type=jnp.float32,
        )
        fock_win = fock_win.reshape(PERTS, WINDOW, row_share, WINDOW * BLOCK)
        for offset in range(WINDOW):
            lead_block = REACH - offset
            place_at = (local_starts[batch_no] + offset, 0, 0, lead_block * BLOCK)
            present = lax.dynamic_slice(running, place_at, (1, PERTS, row_share, WINDOW * BLOCK))
            running = lax.dynamic_update_slice(
                running, present + fock_win[:, offset][None], place_at
            )
        return running

    return lax.fori_loop(0, phi_all.shape[0], add_batch, running)


def shards(density, basis_vals, kernel, starts, counts, pair_mask):
    blk_dev = density.shape[0]
    row_share = density.shape[2]
    grid_pos = lax.axis_index("grid")
    basis_pos = lax.axis_index("basis")
    hops = (REACH + blk_dev - 1) // blk_dev
    wide_rows = blk_dev + 2 * REACH
    cut_rows = hops * blk_dev - REACH
    first_block = grid_pos * blk_dev - REACH
    mask_padded = jnp.pad(pair_mask, ((REACH, REACH), (0, 0)))
    mask_local = lax.dynamic_slice_in_dim(mask_padded, grid_pos * blk_dev, wide_rows, 0)
    mask_wide = jnp.repeat(mask_local, BLOCK, axis=1)
    local_starts = starts - first_block
    positions = jnp.arange(POINTS, dtype=jnp.int32)
    live_points = (positions[None, :] < counts[:, None]).astype(jnp.float32)
    below = [passed_along(density, "grid", dist) for dist in range(1, hops + 1)]
    above = [passed_along(density, "grid", -dist) for dist in range(1, hops + 1)]
    stacked = jnp.concatenate(below[::-1] + [density] + above, axis=0)
    extended = stacked[cut_rows : cut_rows + wide_rows]
    masked = extended * mask_wide[:, None, None, :].astype(jnp.bfloat16)
    row_first = basis_pos * row_share
    density_part = partial_densities(masked, basis_vals, local_starts, row_first, row_share)
    rho = lax.psum(density_part, "basis")
    potential = kernel[:, None, :] * rho * live_points[:, None, :]
    fock_wide = accumulate(wide_rows, basis_vals, local_starts, potential, row_first, row_share)
    padded = jnp.pad(fock_wide, ((cut_rows, cut_rows), (0, 0), (0, 0), (0, 0)))
    pieces = padded.reshape((2 * hops + 1, blk_dev) + fock_wide.shape[1:])
    owned_rows = pieces[hops]
    for dist in range(1, hops + 1):
        owned_rows = owned_rows + passed_along(pieces[hops + dist], "grid", dist)
        owned_rows = owned_rows + passed_along(pieces[hops - dist], "grid", -dist)
    keep_mask = mask_wide[REACH : REACH + blk_dev].astype(jnp.float32)
    return owned_rows * keep_mask[:, None, None, :]


def solution(mesh):
    placed = (
        P("grid", None, "basis", None),
        P("grid", None, None),
        P("grid", None),
        P("grid"),
        P("grid"),
        P(),
    )
    return jax.shard_map(
        shards,
        mesh=mesh,
        in_specs=placed,
        out_specs=P("grid", None, "basis", None),
        check_vma=False,
    )
```

profile of v0, /device:TPU:5, one launch (start us, length us, event | category | flops | bytes accessed | tf_op | source)
XLA Modules:
  0.0 915.8 jit_solution(1660886965244795781)
XLA Ops:
  6.5 5.5 collective-permute-start
  18.7 5.1 collective-permute-start.4
  23.8 39.7 %collective-permute-done = bf16[2,12,32,1408]{3,2,1,0:T(8,128)(2,1)} collective-permute-done((bf16[2,12,32,1408]{3,2,1,0:T(8,128)(2,1)}, bf16[2,12,32,1408]{3,2,1,0:T(8,128)(2,1)}, u32[]{:S(2)}, u32[]{:S(2)}) %collective-permute-start) | collective-permute-done | bytes 2162720 | tf_op jit(solution)/shard_map/ppermute | solution.py:17
  66.4 3.2 copy.36
  71.4 39.5 %collective-permute-done.1 = bf16[2,12,32,1408]{3,2,1,0:T(8,128)(2,1)} collective-permute-done((bf16[2,12,32,1408]{3,2,1,0:T(8,128)(2,1)}, bf16[2,12,32,1408]{3,2,1,0:T(8,128)(2,1)}, u32[]{:S(2)}, u32[]{:S(2)}) %collective-permute-start.1) | collective-permute-done | bytes 2162720 | tf_op jit(solution)/shard_map/ppermute | solution.py:17
  112.8 14.4 %collective-permute-done.2 = bf16[2,12,32,1408]{3,2,1,0:T(8,128)(2,1)} collective-permute-done((bf16[2,12,32,1408]{3,2,1,0:T(8,128)(2,1)}, bf16[2,12,32,1408]{3,2,1,0:T(8,128)(2,1)}, u32[]{:S(2)}, u32[]{:S(2)}) %collective-permute-start.2) | collective-permute-done | bytes 2162720 | tf_op jit(solution)/shard_map/ppermute | solution.py:17
  133.3 23.9 %collective-permute-done.5 = bf16[2,12,32,1408]{3,2,1,0:T(8,128)(2,1)} collective-permute-done((bf16[2,12,32,1408]{3,2,1,0:T(8,128)(2,1)}, bf16[2,12,32,1408]{3,2,1,0:T(8,128)(2,1)}, u32[]{:S(2)}, u32[]{:S(2)}) %collective-permute-start.5) | collective-permute-done | bytes 2162720 | tf_op jit(solution)/shard_map/ppermute | solution.py:17
  159.1 5.5 slice_multiply_fusion
  164.6 90.8 %while.27 = (s32[]{:T(128)}, f32[8,12,256]{2,1,0:T(8,128)}, bf16[8,256,768]{1,2,0:T(8,128)(2,1)S(1)}, s32[]{:T(128)}, s32[8]{0:T(128)S(1)}, /*index=5*/bf16[12,1...) while((s32[]{:T(128)}, f32[8,12,256]{2,1,0:T(8,128)}, ...), condition=%wide.region_2.3_spmd, body=%wide.region_0.2_spmd.sunk | while | flops 907195392 | bytes 19603860 | solution.py:50
  255.5 60.8 %all-reduce.4.cloned.1.call-done = f32[8,12,256]{2,1,0:T(8,128)} async-done(((f32[8,12,256]{2,1,0:T(8,128)}), f32[8,12,256]{2,1,0:T(8,128)}) %all-reduce.4.cloned.1.call-update) | async-done | bytes 98320 | tf_op jit(solution)/shard_map/psum | solution.py:102
  317.3 11.8 %broadcast_in_dim.23 = f32[12,12,32,1408]{3,2,1,0:T(8,128)} broadcast(f32[]{:T(128)} %constant.185.clone.1), dimensions={} | broadcast | bytes 25952260 | tf_op jit(solution)/shard_map/broadcast_in_dim | solution.py:54
  329.1 219.9 %while.28 = (s32[]{:T(128)}, f32[12,12,32,1408]{3,2,1,0:T(8,128)}, s32[8]{0:T(128)S(1)}, f32[8,12,256]{2,1,0:T(8,128)S(1)}, bf16[8,256,768]{1,2,0:T(8,128)(2,1)S...) while((s32[]{:T(128)}, f32[12,12,32,1408]{3,2,1,0:T(8,128)}, ...), condition=%wide.region_5.6_spmd, body=%wide.region_4.5_spmd.sunk | while | flops 5438226432 | bytes 30216672 | solution.py:77
  338.2 3.3 fusion.59
  365.6 3.3 fusion.59
  393.2 3.3 fusion.59
  420.7 3.3 fusion.59
  448.1 3.3 fusion.59
  475.6 3.3 fusion.59
  486.4 2.6 fusion.63
  503.1 3.3 fusion.59
  530.7 3.3 fusion.59
  549.0 15.5 %fusion.28 = (f32[2,12,32,1408]{3,2,1,0:T(8,128)S(1)}, f32[2,12,32,1408]{3,2,1,0:T(8,128)}, f32[2,12,32,1408]{3,2,1,0:T(8,128)}, f32[2,12,32,1408]{3,2,1,0:T(8,1...) fusion(f32[12,12,32,1408]{3,2,1,0:T(8,128)} %get-tuple-element.242), kind=kLoop, calls=%fused_computation.67 | loop fusion | bytes 69206016 | tf_op jit(solution)/shard_map/slice | solution.py:109
  564.5 5.9 collective-permute-start.6
  570.4 2.6 collective-permute-start.11
  573.0 4.5 collective-permute-start.10
  577.5 5.1 collective-permute-start.9
  584.5 119.2 %collective-permute-done.6 = f32[2,12,32,1408]{3,2,1,0:T(8,128)} collective-permute-done((f32[2,12,32,1408]{3,2,1,0:T(8,128)S(1)}, f32[2,12,32,1408]{3,2,1,0:T(8,128)}, u32[]{:S(2)}, u32[]{:S(2)}) %collective-permute-start.6) | collective-permute-done | bytes 4325408 | tf_op jit(solution)/shard_map/ppermute | solution.py:17
  703.7 50.7 %collective-permute-start.7 = (f32[2,12,32,1408]{3,2,1,0:T(8,128)}, f32[2,12,32,1408]{3,2,1,0:T(8,128)}, u32[]{:S(2)}, u32[]{:S(2)}) collective-permute-start(f32[2,12,32,1408]{3,2,1,0:T(8,128)} %get-tuple-element.296), channel_id=1, source_target_pairs={{4,0},{8,4},{12,8},{16,12},{20,16},{24,20},{28,24},{32,28},{36,32}... | collective-permute-start | bytes 12976136 | tf_op jit(solution)/shard_map/ppermute | solution.py:17
  754.6 41.9 %collective-permute-done.10 = f32[2,12,32,1408]{3,2,1,0:T(8,128)} collective-permute-done((f32[2,12,32,1408]{3,2,1,0:T(8,128)}, f32[2,12,32,1408]{3,2,1,0:T(8,128)}, u32[]{:S(2)}, u32[]{:S(2)}) %collective-permute-start.10) | collective-permute-done | bytes 4325408 | tf_op jit(solution)/shard_map/ppermute | solution.py:17
  796.5 56.3 %collective-permute-done.9 = f32[2,12,32,1408]{3,2,1,0:T(8,128)} collective-permute-done((f32[2,12,32,1408]{3,2,1,0:T(8,128)}, f32[2,12,32,1408]{3,2,1,0:T(8,128)}, u32[]{:S(2)}, u32[]{:S(2)}) %collective-permute-start.9) | collective-permute-done | bytes 4325408 | tf_op jit(solution)/shard_map/ppermute | solution.py:17
  852.8 42.9 %collective-permute-done.8 = f32[2,12,32,1408]{3,2,1,0:T(8,128)} collective-permute-done((f32[2,12,32,1408]{3,2,1,0:T(8,128)}, f32[2,12,32,1408]{3,2,1,0:T(8,128)}, u32[]{:S(2)}, u32[]{:S(2)}) %collective-permute-start.8) | collective-permute-done | bytes 4325408 | tf_op jit(solution)/shard_map/ppermute | solution.py:17
  895.8 13.2 %add_multiply_fusion = f32[2,12,32,1408]{3,2,1,0:T(8,128)} fusion(f32[2,12,32,1408]{3,2,1,0:T(8,128)} %collective-permute-done.11, f32[2,12,32,1408]{3,2,1,0:T(8,128)} %collective-permute-done.10, f32[2,12,32,1408]{3,2,1,0:T(8,128)} %collective-permute-done.9, f32[2,12,32,1408]{3,2,1,0:T(8,128)} %collective-permute-done.8, ...), kind=kLoop, calls=%fused_computation.49 | loop fusion | flops 7569408 | bytes 34614272 | tf_op jit(solution)/shard_map/mul | solution.py:112
  (229 shorter events, 223.2 us)
Async XLA Ops:
  6.5 63.0 %copy-start.3 = (s32[8]{0:T(128)S(1)}, s32[8]{0:T(128)}, u32[]{:S(2)}) copy-start(s32[8]{0:T(128)} %param.13) | copy-start | bytes 100
  6.5 309.8 %all-reduce.4.cloned.1.call-start = ((), (), s32[]{:S(2)}) async-start(), calls=%async_computation | async-start | bytes 262144 | tf_op jit(solution)/shard_map/psum | solution.py:102
  6.5 56.9 %collective-permute-start = (bf16[2,12,32,1408]{3,2,1,0:T(8,128)(2,1)}, bf16[2,12,32,1408]{3,2,1,0:T(8,128)(2,1)}, u32[]{:S(2)}, u32[]{:S(2)}) collective-permute-start(bf16[2,12,32,1408]{3,2,1,0:T(8,128)(2,1)} %param.10), channel_id=1, source_target_pairs={{0,12},{4,16},{8,20},{12,24},{16,28},{20,32},{24,36},{28,40},{32,4... | collective-permute-start | bytes 6488072 | tf_op jit(solution)/shard_map/ppermute | solution.py:17
  12.1 98.8 %collective-permute-start.1 = (bf16[2,12,32,1408]{3,2,1,0:T(8,128)(2,1)}, bf16[2,12,32,1408]{3,2,1,0:T(8,128)(2,1)}, u32[]{:S(2)}, u32[]{:S(2)}) collective-permute-start(bf16[2,12,32,1408]{3,2,1,0:T(8,128)(2,1)} %param.10), channel_id=1, source_target_pairs={{0,8},{4,12},{8,16},{12,20},{16,24},{20,28},{24,32},{28,36},{32,40... | collective-permute-start | bytes 6488072 | tf_op jit(solution)/shard_map/ppermute | solution.py:17
  14.4 112.7 %collective-permute-start.2 = (bf16[2,12,32,1408]{3,2,1,0:T(8,128)(2,1)}, bf16[2,12,32,1408]{3,2,1,0:T(8,128)(2,1)}, u32[]{:S(2)}, u32[]{:S(2)}) collective-permute-start(bf16[2,12,32,1408]{3,2,1,0:T(8,128)(2,1)} %param.10), channel_id=1, source_target_pairs={{0,4},{4,8},{8,12},{12,16},{16,20},{20,24},{24,28},{28,32},{32,36}... | collective-permute-start | bytes 6488072 | tf_op jit(solution)/shard_map/ppermute | solution.py:17
  16.6 112.8 %collective-permute-start.3 = (bf16[2,12,32,1408]{3,2,1,0:T(8,128)(2,1)}, bf16[2,12,32,1408]{3,2,1,0:T(8,128)(2,1)}, u32[]{:S(2)}, u32[]{:S(2)}) collective-permute-start(bf16[2,12,32,1408]{3,2,1,0:T(8,128)(2,1)} %param.10), channel_id=1, source_target_pairs={{4,0},{8,4},{12,8},{16,12},{20,16},{24,20},{28,24},{32,28},{36,32}... | collective-permute-start | bytes 6488072 | tf_op jit(solution)/shard_map/ppermute | solution.py:17
  18.7 112.6 %collective-permute-start.4 = (bf16[2,12,32,1408]{3,2,1,0:T(8,128)(2,1)}, bf16[2,12,32,1408]{3,2,1,0:T(8,128)(2,1)}, u32[]{:S(2)}, u32[]{:S(2)}) collective-permute-start(bf16[2,12,32,1408]{3,2,1,0:T(8,128)(2,1)} %param.10), channel_id=1, source_target_pairs={{8,0},{12,4},{16,8},{20,12},{24,16},{28,20},{32,24},{36,28},{40,32... | collective-permute-start | bytes 6488072 | tf_op jit(solution)/shard_map/ppermute | solution.py:17
  63.5 93.7 %collective-permute-start.5 = (bf16[2,12,32,1408]{3,2,1,0:T(8,128)(2,1)}, bf16[2,12,32,1408]{3,2,1,0:T(8,128)(2,1)}, u32[]{:S(2)}, u32[]{:S(2)}) collective-permute-start(bf16[2,12,32,1408]{3,2,1,0:T(8,128)(2,1)} %param.10), channel_id=1, source_target_pairs={{12,0},{16,4},{20,8},{24,12},{28,16},{32,20},{36,24},{40,28},{44,3... | collective-permute-start | bytes 6488072 | tf_op jit(solution)/shard_map/ppermute | solution.py:17
  71.3 57.7 %copy-start = (bf16[2,12,32,1408]{3,2,1,0:T(8,128)(2,1)S(1)}, bf16[2,12,32,1408]{3,2,1,0:T(8,128)(2,1)}, u32[]{:S(2)}) copy-start(bf16[2,12,32,1408]{3,2,1,0:T(8,128)(2,1)} %param.10) | copy-start | bytes 6488068
  164.6 90.8 %copy-start.2 = (s32[8]{0:T(128)S(1)}, s32[8]{0:T(128)}, u32[]{:S(2)}) copy-start(s32[8]{0:T(128)} %param.14) | copy-start | bytes 100
  164.6 151.8 %copy-start.1 = (f32[8,256]{1,0:T(8,128)S(1)}, f32[8,256]{1,0:T(8,128)}, u32[]{:S(2)}) copy-start(f32[8,256]{1,0:T(8,128)} %param.12) | copy-start | bytes 24580
  564.5 139.2 %collective-permute-start.6 = (f32[2,12,32,1408]{3,2,1,0:T(8,128)S(1)}, f32[2,12,32,1408]{3,2,1,0:T(8,128)}, u32[]{:S(2)}, u32[]{:S(2)}) collective-permute-start(f32[2,12,32,1408]{3,2,1,0:T(8,128)S(1)} %get-tuple-element.291), channel_id=1, source_target_pairs={{0,4},{4,8},{8,12},{12,16},{16,20},{20,24},{24,28},{28,32},{32,36}... | collective-permute-start | bytes 12976136 | tf_op jit(solution)/shard_map/ppermute | solution.py:17
  570.4 184.2 %collective-permute-start.11 = (f32[2,12,32,1408]{3,2,1,0:T(8,128)}, f32[2,12,32,1408]{3,2,1,0:T(8,128)}, u32[]{:S(2)}, u32[]{:S(2)}) collective-permute-start(f32[2,12,32,1408]{3,2,1,0:T(8,128)} %get-tuple-element.292), channel_id=1, source_target_pairs={{12,0},{16,4},{20,8},{24,12},{28,16},{32,20},{36,24},{40,28},{44,3... | collective-permute-start | bytes 12976136 | tf_op jit(solution)/shard_map/ppermute | solution.py:17
  573.0 223.5 %collective-permute-start.10 = (f32[2,12,32,1408]{3,2,1,0:T(8,128)}, f32[2,12,32,1408]{3,2,1,0:T(8,128)}, u32[]{:S(2)}, u32[]{:S(2)}) collective-permute-start(f32[2,12,32,1408]{3,2,1,0:T(8,128)} %get-tuple-element.293), channel_id=1, source_target_pairs={{0,12},{4,16},{8,20},{12,24},{16,28},{20,32},{24,36},{28,40},{32,4... | collective-permute-start | bytes 12976136 | tf_op jit(solution)/shard_map/ppermute | solution.py:17
  577.5 275.3 %collective-permute-start.9 = (f32[2,12,32,1408]{3,2,1,0:T(8,128)}, f32[2,12,32,1408]{3,2,1,0:T(8,128)}, u32[]{:S(2)}, u32[]{:S(2)}) collective-permute-start(f32[2,12,32,1408]{3,2,1,0:T(8,128)} %get-tuple-element.294), channel_id=1, source_target_pairs={{8,0},{12,4},{16,8},{20,12},{24,16},{28,20},{32,24},{36,28},{40,32... | collective-permute-start | bytes 12976136 | tf_op jit(solution)/shard_map/ppermute | solution.py:17
  582.6 313.2 %collective-permute-start.8 = (f32[2,12,32,1408]{3,2,1,0:T(8,128)}, f32[2,12,32,1408]{3,2,1,0:T(8,128)}, u32[]{:S(2)}, u32[]{:S(2)}) collective-permute-start(f32[2,12,32,1408]{3,2,1,0:T(8,128)} %get-tuple-element.295), channel_id=1, source_target_pairs={{0,8},{4,12},{8,16},{12,20},{16,24},{20,28},{24,32},{28,36},{32,40... | collective-permute-start | bytes 12976136 | tf_op jit(solution)/shard_map/ppermute | solution.py:17
  703.7 192.1 %collective-permute-start.7 = (f32[2,12,32,1408]{3,2,1,0:T(8,128)}, f32[2,12,32,1408]{3,2,1,0:T(8,128)}, u32[]{:S(2)}, u32[]{:S(2)}) collective-permute-start(f32[2,12,32,1408]{3,2,1,0:T(8,128)} %get-tuple-element.296), channel_id=1, source_target_pairs={{4,0},{8,4},{12,8},{16,12},{20,16},{24,20},{28,24},{32,28},{36,32}... | collective-permute-start | bytes 12976136 | tf_op jit(solution)/shard_map/ppermute | solution.py:17
Sparse Core Ops, SparseCore 0:
  255.5 60.7 all-reduce.3
where the time goes:
time: 922 us; the launch traced here: 916 us
  waiting for transfers between devices  439 us (48%)
  other arithmetic  141 us (15%)
  local copies, waits for them, and re-layouts  115 us (12%)
  starting transfers between devices  89.8 us (10%)
  loops' own time  82.9 us (9%)
  matrix products  35.5 us (4%)
  between operations  13.7 us (1%)
    ppermute x12, waiting for transfers between devices, passed_along(): return lax.ppermute(block, axis, route)  378 us
    dynamic_update_slice x48, other arithmetic, add_batch(): lax.dynamic_update_slice(running, present + fock_win[:, offset][None], pl...  121 us
    ppermute x12, starting transfers between devices, passed_along(): return lax.ppermute(block, axis, route)  89.8 us
    another operation x1, loops' own time, accumulate(): return lax.fori_loop(0, phi_all.shape[0], add_batch, running)  67.7 us
    psum x1, waiting for transfers between devices, shards(): rho = lax.psum(density_part, 'basis')  60.8 us
    while x40, local copies, waits for them, and re-layouts  44.5 us
    dot_general x8, matrix products, add_batch(): jnp.einsum('kpr,pc->krc', weighted, phi_vals.astype(jnp.float32), precisi...  26.4 us
  transfers between devices with their start and end apart: 13, of which 10 were waited for; matrix products, arithmetic and copies ran while one was open for 2% of the time, Pallas kernels for 0%

commit v1 on v0

v1 whole, which is shorter than its diff:
```python
import functools

import jax
import jax.numpy as jnp
from jax import lax
from jax.experimental import pallas as pl
from jax.experimental.pallas import tpu as pltpu
from jax.sharding import PartitionSpec as P

BLOCK = 128
PERTS = 12
WINDOW = 6
POINTS = 256
REACH = 5
BAND = 11
COLS = WINDOW * BLOCK
WIDE = BAND * BLOCK
SLOTS = 6
MESH = pl.DeviceIdType.MESH
NT = (((1,), (1,)), ((), ()))


def one_hot(share, columns, first):
    rows = lax.broadcasted_iota(jnp.int32, (share, columns), 0)
    lanes = lax.broadcasted_iota(jnp.int32, (share, columns), 1)
    return jnp.where(lanes == rows + first, 1.0, 0.0).astype(jnp.bfloat16)


def density_kernel(
    chips, planes, batches, share,
    phi_ref, meta_ref, dens_ref, starts_ref, counts_ref, mask_ref, kern_ref,
    all_ref, meta_all_ref, pot_ref,
    phi_v, dens_v, far_v, left_v, left_far, meta_s, part, gathered, pot_v,
    own_sem, out_sem, core_s, core_r, y_s, y_r, z_s, z_r, c_s, c_r, m_s, m_r, f_sem, a_s, a_r, b_s, b_r,
):
    grid_pos, plane = lax.axis_index("grid"), lax.axis_index("basis")
    chip, core = grid_pos // 2, lax.rem(grid_pos, 2)
    half = batches // 2
    quarter = half // 2
    per_plane = batches // planes
    own_slot = 2 + core
    first = lax.rem(plane, 2) * half
    there = half - first
    rows_all = PERTS * share

    def device(slot, at_plane):
        return (2 * lax.rem(chip + slot // 2 - 1 + chips, chips) + lax.rem(slot, 2), at_plane)

    other = (2 * chip + 1 - core, plane)

    def remote(src, dst, send, recv, to):
        return pltpu.make_async_remote_copy(
            src_ref=src, dst_ref=dst, send_sem=send, recv_sem=recv, device_id=to, device_id_type=MESH)

    barrier = pltpu.get_barrier_semaphore()

    @pl.loop(0, SLOTS * planes)
    def _(no):
        slot, at_plane = no // planes, lax.rem(no, planes)

        @pl.when(jnp.logical_or(slot != own_slot, at_plane != plane))
        def _():
            pl.semaphore_signal(barrier, inc=1, device_id=device(slot, at_plane), device_id_type=MESH)

    pl.semaphore_wait(barrier, SLOTS * planes - 1)

    def piece(way, n):
        return n // 2 + quarter * lax.rem(n + way, 2)

    def y_copy(way, n):
        at = first + piece(way, n)
        return remote(phi_ref.at[at], phi_v.at[4 * way + core, at], y_s.at[way, n], y_r.at[way, n],
                      device(4 - 4 * way + core, plane))

    def z_copy(way, n):
        which = piece(way, n)
        where = phi_v.at[4 * way + core, first + which]
        to = lax.rem(plane + 1 - 2 * (which // quarter) + planes, planes)
        return remote(where, where, z_s.at[way, n], z_r.at[way, n], (grid_pos, to))

    def c_copy(way, m):
        at = jnp.where(m < half, first, there) + piece(way, lax.rem(m, half))
        where = phi_v.at[4 * way + core, at]
        return remote(where, where, c_s.at[way, m], c_r.at[way, m], other)

    def core_copy(no):
        return remote(phi_ref.at[no], phi_v.at[own_slot, no], core_s.at[no], core_r.at[no], other)

    def meta_copy(way, s):
        return remote(meta_ref, meta_all_ref.at[4 * way + core], m_s.at[1 + 2 * way + s], m_r.at[1 + 2 * way + core],
                      device(4 - 4 * way + s, plane))

    def out_copy(slot, no):
        return pltpu.make_async_copy(phi_v.at[slot, no], all_ref.at[slot, no], out_sem.at[slot, no])

    own_copy = pltpu.make_async_copy(phi_ref, phi_v.at[own_slot], own_sem.at[0])
    own_copy.start()
    far_copy = remote(dens_ref.at[core, :, :, pl.ds(pl.multiple_of(core * REACH * BLOCK, BLOCK), COLS)], left_far,
                      f_sem.at[0], f_sem.at[1], device(jnp.where(core == 0, 1, 4), plane))
    dens_copy = pltpu.make_async_copy(dens_ref, left_v, own_sem.at[1])
    dens_copy.start()
    core_meta = remote(meta_ref, meta_all_ref.at[own_slot], m_s.at[0], m_r.at[0], other)
    core_meta.start()
    for way in range(2):
        for s in range(2):
            meta_copy(way, s).start()
    own_meta = pltpu.make_async_copy(meta_ref, meta_all_ref.at[own_slot], own_sem.at[2])
    own_meta.start()

    @pl.loop(0, half)
    def _(n):
        for way in range(2):
            y_copy(way, n).start()

    far_copy.start()

    @pl.loop(0, batches)
    def _(no):
        core_copy(no).start()

    def masked(block, keep):
        return (block.astype(jnp.float32) * keep.astype(jnp.float32)).astype(block.dtype)

    def same(left, right):
        return (1 - jnp.minimum(jnp.abs(left - right), 1)).astype(jnp.float32)

    dens_copy.wait()
    for r in range(2):
        row = 2 * grid_pos + r
        for t in range(BAND):
            block = left_v[r, :, :, t * BLOCK:(t + 1) * BLOCK].reshape(rows_all, BLOCK)
            dens_v[r, t, :rows_all, :] = masked(block, mask_ref[row, t])
            dens_v[r, t, rows_all:, :] = one_hot(share, BLOCK, (REACH - t) * BLOCK + plane * share)
    far_v[rows_all:, :] = one_hot(share, COLS, core * REACH * BLOCK + plane * share)

    own_copy.wait()
    own_meta.wait()
    for no in range(5):
        pltpu.make_async_copy(meta_ref, meta_all_ref.at[own_slot], m_r.at[no]).wait()
    to_smem = pltpu.make_async_copy(meta_all_ref, meta_s, own_sem.at[3])
    to_smem.start()
    to_smem.wait()

    def reduced(mixed):
        picked = mixed[rows_all:rows_all + share]
        return jnp.sum(mixed[:rows_all].reshape(PERTS, share, POINTS) * picked[None], axis=1)

    def rho_part(slot, no):
        start = meta_s[slot, no, 0]
        phi = phi_v[slot, no]
        lhs, keeps = [], []
        for r in range(2):
            offset = 2 * grid_pos + r - start
            inside = jnp.clip(offset, 0, WINDOW - 1)
            keeps.append(same(offset, inside))
            lhs.append(jnp.concatenate([dens_v[r, REACH - inside + c] for c in range(WINDOW)], axis=1))
        total = None
        for r in range(2):
            mixed = lax.dot_general(lhs[r], phi, NT, preferred_element_type=jnp.float32)
            term = reduced(mixed) * keeps[r]
            total = term if total is None else total + term
        part[slot, no // per_plane, lax.rem(no, per_plane)] = total

    far_start = 4 * chip - 1

    def rho_far(slot, no):
        keep = same(meta_s[slot, no, 0], far_start)
        mixed = lax.dot_general(far_v[...], phi_v[slot, no], NT, preferred_element_type=jnp.float32)
        spot = part.at[slot, no // per_plane, lax.rem(no, per_plane)]
        spot[...] = spot[...] + reduced(mixed) * keep

    @pl.loop(0, batches)
    def _(no):
        out_copy(own_slot, no).start()
        rho_part(own_slot, no)

    @pl.loop(0, batches)
    def _(no):
        core_copy(no).wait_recv()
        out_copy(5 - own_slot, no).start()
        rho_part(5 - own_slot, no)

    def far_ready():
        far_copy.wait_recv()
        far_row = jnp.where(core == 0, jnp.maximum(2 * grid_pos - 1, 0), jnp.minimum(2 * grid_pos + 2, 2 * 2 * chips - 1))
        for t in range(WINDOW):
            block = left_far[:, :, t * BLOCK:(t + 1) * BLOCK].reshape(rows_all, BLOCK)
            far_v[:rows_all, t * BLOCK:(t + 1) * BLOCK] = masked(block, mask_ref[far_row, jnp.where(core == 0, REACH, 0) + t])

    @pl.loop(0, half + 2)
    def _(n):
        y_now = n < half
        z_now = jnp.logical_and(n >= 1, n <= half)
        cz_now = n >= 2

        @pl.when(y_now)
        def _():
            for way in range(2):
                y_copy(way, n).wait_recv()
                z_copy(way, n).start()
                c_copy(way, n).start()
                out_copy(4 * way + core, first + piece(way, n)).start()

        @pl.when(n == 0)
        def _():
            far_ready()

        @pl.when(z_now)
        def _():
            for way in range(2):
                z_copy(way, n - 1).wait_recv()
                c_copy(way, half + n - 1).start()
                out_copy(4 * way + core, there + piece(way, n - 1)).start()
            for way in range(2):
                c_copy(way, n - 1).wait_recv()
                out_copy(4 * way + 1 - core, first + piece(way, n - 1)).start()

        @pl.when(cz_now)
        def _():
            for way in range(2):
                c_copy(way, half + n - 2).wait_recv()
                out_copy(4 * way + 1 - core, there + piece(way, n - 2)).start()

        @pl.loop(0, 8)
        def _(item):
            kind, way = item // 2, lax.rem(item, 2)
            late = jnp.where(kind == 0, 0, jnp.where(kind == 3, 2, 1))
            came = n - late
            slot = 4 * way + jnp.where(kind <= 1, core, 1 - core)
            at = jnp.where(lax.rem(kind, 2) == 0, first, there) + piece(way, jnp.maximum(came, 0))

            @pl.when(jnp.logical_and(came >= 0, came < half))
            def _():
                rho_part(slot, at)

                @pl.when(jnp.logical_and(kind <= 1, way == 1 - core))
                def _():
                    rho_far(slot, at)

    def is_other(slot, at_plane):
        return jnp.logical_or(slot != own_slot, at_plane != plane)

    def part_copy(slot, at_plane):
        back = 2 * (2 - slot // 2) + core
        return remote(part.at[slot, at_plane], gathered.at[back, plane], a_s.at[slot, at_plane], a_r.at[back, plane],
                      device(slot, at_plane))

    def pot_copy(slot, at_plane):
        back = 2 * (2 - slot // 2) + core
        return remote(pot_v, pot_ref.at[back, plane], b_s.at[slot, at_plane], b_r.at[back, plane],
                      device(slot, at_plane))

    def for_others(act):
        @pl.loop(0, SLOTS * planes)
        def _(no):
            slot, at_plane = no // planes, lax.rem(no, planes)

            @pl.when(is_other(slot, at_plane))
            def _():
                act(slot, at_plane)

    for_others(lambda slot, at_plane: part_copy(slot, at_plane).start())
    gathered[own_slot, plane] = part[own_slot, plane]
    for_others(lambda slot, at_plane: pltpu.make_async_copy(
        part.at[0, 0], gathered.at[slot, at_plane], a_r.at[slot, at_plane]).wait())
    points = lax.broadcasted_iota(jnp.int32, (1, POINTS), 1)
    for no in range(per_plane):
        rho = gathered[0, 0, no]
        for slot in range(SLOTS):
            for at_plane in range(planes):
                if slot or at_plane:
                    rho = rho + gathered[slot, at_plane, no]
        mine = per_plane * plane + no
        live = jnp.clip(counts_ref[mine] - points, 0, 1).astype(jnp.float32)
        pot_v[no] = rho * (kern_ref[pl.ds(mine, 1), :] * live)
    for_others(lambda slot, at_plane: pot_copy(slot, at_plane).start())
    pot_own = pltpu.make_async_copy(pot_v, pot_ref.at[own_slot, plane], own_sem.at[0])
    pot_own.start()
    for_others(lambda slot, at_plane: pltpu.make_async_copy(
        pot_v, pot_ref.at[slot, at_plane], b_r.at[slot, at_plane]).wait())
    pot_own.wait()

    for_others(lambda slot, at_plane: part_copy(slot, at_plane).wait_send())
    for_others(lambda slot, at_plane: pot_copy(slot, at_plane).wait_send())
    far_copy.wait_send()
    core_meta.wait_send()
    for way in range(2):
        for s in range(2):
            meta_copy(way, s).wait_send()

    @pl.loop(0, batches)
    def _(no):
        core_copy(no).wait_send()
        for slot in range(SLOTS):
            out_copy(slot, no).wait()

    @pl.loop(0, half)
    def _(n):
        for way in range(2):
            y_copy(way, n).wait_send()
            z_copy(way, n).wait_send()
            c_copy(way, n).wait_send()
            c_copy(way, half + n).wait_send()


def potentials(phi, meta, density, starts, counts, pair_mask, kern, chips, planes):
    batches, points, cols = phi.shape
    share = density.shape[2]
    half, per_plane = batches // 2, batches // planes
    rows = PERTS * share + share
    far = pl.BlockSpec(memory_space=pl.ANY)
    smem = pl.BlockSpec(memory_space=pltpu.SMEM)
    vmem = pl.BlockSpec(memory_space=pltpu.VMEM)
    dma = pltpu.SemaphoreType.DMA
    f32 = jnp.float32
    small = (SLOTS, planes, per_plane, PERTS, points)
    return pl.pallas_call(
        functools.partial(density_kernel, chips, planes, batches, share),
        out_shape=(
            jax.ShapeDtypeStruct((SLOTS, batches, points, cols), phi.dtype),
            jax.ShapeDtypeStruct((SLOTS,) + meta.shape, meta.dtype),
            jax.ShapeDtypeStruct(small, f32),
        ),
        in_specs=[far, far, far, smem, smem, smem, vmem],
        out_specs=[far] * 3,
        scratch_shapes=[
            pltpu.VMEM((SLOTS, batches, points, cols), phi.dtype),
            pltpu.VMEM((2, BAND, rows, BLOCK), density.dtype),
            pltpu.VMEM((rows, COLS), density.dtype),
            pltpu.VMEM(density.shape, density.dtype),
            pltpu.VMEM((PERTS, share, COLS), density.dtype),
            pltpu.SMEM((SLOTS,) + meta.shape, meta.dtype),
            pltpu.VMEM(small, f32),
            pltpu.VMEM(small, f32),
            pltpu.VMEM((per_plane, PERTS, points), f32),
            dma((4,)), dma((SLOTS, batches)), dma((batches,)), dma((batches,)),
            dma((2, half)), dma((2, half)), dma((2, half)), dma((2, half)),
            dma((2, batches)), dma((2, batches)), dma((5,)), dma((5,)), dma((2,)),
            dma((SLOTS, planes)), dma((SLOTS, planes)), dma((SLOTS, planes)), dma((SLOTS, planes)),
        ],
        compiler_params=pltpu.CompilerParams(collective_id=0, has_side_effects=True, vmem_limit_bytes=56 << 20),
        cost_estimate=pl.CostEstimate(flops=17 * 10**9, bytes_accessed=50 * 10**6, transcendentals=0),
        name="potentials",
    )(phi, meta, density, starts, counts, pair_mask, kern)


def split_weights(pot, picked, share):
    weighted = (pot[:, None, :] * picked[None]).reshape(PERTS * share, POINTS)
    high = weighted.astype(jnp.bfloat16)
    low = (weighted - high.astype(jnp.float32)).astype(jnp.bfloat16)
    return high, low


def add_product(parts, phi, few, store):
    def product(points):
        left = jnp.concatenate(
            [jnp.concatenate([high[:, :points], low[:, :points]], axis=1) for high, low in parts], axis=0)
        right = phi[:points, :]
        store(jnp.dot(left, jnp.concatenate([right, right], axis=0), preferred_element_type=jnp.float32))

    @pl.when(few)
    def _():
        product(POINTS // 2)

    @pl.when(jnp.logical_not(few))
    def _():
        product(POINTS)


DEPTH = 4


def fock_kernel(batches, share, meta_ref, mask_ref, pot_ref, phi_ref, out_ref, chosen, buf, sems):
    grid_pos, plane = lax.axis_index("grid"), lax.axis_index("basis")
    base = 2 * grid_pos - REACH

    def note(no, count):
        lead = meta_ref[no // batches, lax.rem(no, batches), 0] - base
        near = jnp.logical_and(lead >= 0, lead <= REACH + 1)

        @pl.when(near)
        def _():
            chosen[count] = no

        return count + near.astype(jnp.int32)

    count = lax.fori_loop(0, SLOTS * batches, note, 0)

    def fetch(i):
        no = chosen[i]
        return pltpu.make_async_copy(
            phi_ref.at[no // batches, lax.rem(no, batches)], buf.at[lax.rem(i, DEPTH)], sems.at[lax.rem(i, DEPTH)])

    for i in range(DEPTH - 1):
        @pl.when(i < count)
        def _():
            fetch(i).start()

    out_ref[...] = jnp.zeros_like(out_ref)
    pick = one_hot(share, BLOCK, plane * share)

    @pl.loop(0, count)
    def _(i):
        fetch(i).wait()

        @pl.when(i + DEPTH - 1 < count)
        def _():
            fetch(i + DEPTH - 1).start()

        no = chosen[i]
        lead = meta_ref[no // batches, lax.rem(no, batches), 0] - base
        few = meta_ref[no // batches, lax.rem(no, batches), 1] <= POINTS // 2
        here = buf.at[lax.rem(i, DEPTH)]
        pot = pot_ref[no]

        def weights(offset):
            own = here[:, pl.ds(pl.multiple_of(offset * BLOCK, BLOCK), BLOCK)]
            picked = lax.dot_general(pick, own, NT, preferred_element_type=jnp.float32)
            return split_weights(pot, picked, share)

        def add(r, offset, value):
            spot = out_ref.at[r, :, :, pl.ds(pl.multiple_of((REACH - offset) * BLOCK, BLOCK), COLS)]
            spot[...] = spot[...] + value.reshape(PERTS, share, COLS)

        both = jnp.logical_and(lead >= 1, lead <= REACH)

        @pl.when(both)
        def _():
            offset = REACH - lead
            parts = [weights(offset), weights(offset + 1)]
            rows = PERTS * share

            def store(value):
                add(0, offset, value[:rows])
                add(1, offset + 1, value[rows:])

            add_product(parts, here, few, store)

        @pl.when(jnp.logical_not(both))
        def _():
            r = jnp.where(lead == 0, 0, 1)
            offset = jnp.where(lead == 0, REACH, 0)
            add_product([weights(offset)], here, few, lambda value: add(r, offset, value))

    for r in range(2):
        for t in range(BAND):
            @pl.when(mask_ref[2 * grid_pos + r, t] == 0)
            def _():
                out_ref[r, :, :, t * BLOCK:(t + 1) * BLOCK] = jnp.zeros((PERTS, share, BLOCK), jnp.float32)


def fock_own(meta_all, pair_mask, pot, phi_all, share):
    slots, batches, points, cols = phi_all.shape
    smem = pl.BlockSpec(memory_space=pltpu.SMEM)
    vmem = pl.BlockSpec(memory_space=pltpu.VMEM)
    return pl.pallas_call(
        functools.partial(fock_kernel, batches, share),
        out_shape=jax.ShapeDtypeStruct((2, PERTS, share, WIDE), jnp.float32),
        in_specs=[smem, smem, vmem, pl.BlockSpec(memory_space=pl.ANY)],
        out_specs=vmem,
        scratch_shapes=[
            pltpu.SMEM((slots * batches,), jnp.int32),
            pltpu.VMEM((DEPTH, points, cols), phi_all.dtype),
            pltpu.SemaphoreType.DMA((DEPTH,)),
        ],
        compiler_params=pltpu.CompilerParams(vmem_limit_bytes=56 << 20),
        cost_estimate=pl.CostEstimate(flops=20 * 10**9, bytes_accessed=20 * 10**6, transcendentals=0),
        name="fock_own",
    )(meta_all, pair_mask, pot, phi_all)


def far_kernel(batches, share, meta_ref, pot_ref, phi_ref, out_ref, buf, sem):
    grid_pos, plane = lax.axis_index("grid"), lax.axis_index("basis")
    core = lax.rem(grid_pos, 2)
    slot = jnp.where(core == 0, 4, 1)
    far_start = 4 * (grid_pos // 2) - 1
    out_ref[...] = jnp.zeros_like(out_ref)
    pick = one_hot(share, BLOCK, plane * share)

    @pl.loop(0, batches)
    def _(no):
        @pl.when(meta_ref[slot, no, 0] == far_start)
        def _():
            copy = pltpu.make_async_copy(phi_ref.at[slot, no], buf, sem)
            copy.start()
            copy.wait()
            own = buf[:, pl.ds(pl.multiple_of(core * REACH * BLOCK, BLOCK), BLOCK)]
            picked = lax.dot_general(pick, own, NT, preferred_element_type=jnp.float32)
            parts = [split_weights(pot_ref[slot * batches + no], picked, share)]

            def store(value):
                out_ref[...] += value.reshape(PERTS, share, COLS)

            add_product(parts, buf, meta_ref[slot, no, 1] <= POINTS // 2, store)


def fock_far(meta_all, pot, phi_all, share):
    slots, batches, points, cols = phi_all.shape
    smem = pl.BlockSpec(memory_space=pltpu.SMEM)
    vmem = pl.BlockSpec(memory_space=pltpu.VMEM)
    return pl.pallas_call(
        functools.partial(far_kernel, batches, share),
        out_shape=jax.ShapeDtypeStruct((PERTS, share, COLS), jnp.float32),
        in_specs=[smem, vmem, pl.BlockSpec(memory_space=pl.ANY)],
        out_specs=vmem,
        scratch_shapes=[pltpu.VMEM((points, cols), phi_all.dtype), pltpu.SemaphoreType.DMA],
        compiler_params=pltpu.CompilerParams(vmem_limit_bytes=56 << 20),
        cost_estimate=pl.CostEstimate(flops=10**9, bytes_accessed=2 * 10**6, transcendentals=0),
        name="fock_far",
    )(meta_all, pot, phi_all)


def shards(density, basis_vals, kernel, starts, counts, pair_mask):
    grid_size, planes = lax.axis_size("grid"), lax.axis_size("basis")
    batches, share = basis_vals.shape[0], density.shape[2]
    grid_pos = lax.axis_index("grid")
    core = lax.rem(grid_pos, 2)
    meta = jnp.pad(jnp.stack([starts, counts], axis=1), ((0, 0), (0, BLOCK - 2)))
    phi_all, meta_all, pot = potentials(
        basis_vals, meta, density, starts, counts, pair_mask, kernel, grid_size // 2, planes)
    pot = pot.reshape(SLOTS * batches, PERTS, POINTS)
    far = fock_far(meta_all, pot, phi_all, share)
    route = [(i, (i + 1) % grid_size if i % 2 else (i - 1) % grid_size) for i in range(grid_size)]
    arrived = lax.ppermute(far, "grid", route)
    own = fock_own(meta_all, pair_mask, pot, phi_all, share)
    mask_row = lax.dynamic_slice(pair_mask, (2 * grid_pos + core, core * REACH), (1, WINDOW))[0]
    keep = jnp.repeat(mask_row, BLOCK).astype(jnp.float32)
    place = (core, 0, 0, core * REACH * BLOCK)
    present = lax.dynamic_slice(own, place, (1, PERTS, share, COLS))
    return lax.dynamic_update_slice(own, present + (arrived * keep)[None], place)


def solution(mesh):
    placed = (
        P("grid", None, "basis", None),
        P("grid", None, None),
        P("grid", None),
        P("grid"),
        P("grid"),
        P(),
    )
    return jax.shard_map(
        shards,
        mesh=mesh,
        in_specs=placed,
        out_specs=P("grid", None, "basis", None),
        check_vma=False,
    )
```

time: 922 us -> 158 us (0.17)
  the two profiles are of different devices: /device:TPU:5 before, /device:TPU:9 now
where the time goes in v1:
time: 158 us; the launch traced here: 156 us
  Pallas kernels  146 us (92%)
  starting transfers between devices  5.36 us (3%)
  other arithmetic  3.3 us (2%)
  local copies, waits for them, and re-layouts  2.16 us (1%)
    pallas_call x1, Pallas kernels, potentials(): pl.pallas_call(functools.partial(density_kernel, chips, planes, batches,...  109 us
    pallas_call x1, Pallas kernels, fock_own(): pl.pallas_call(functools.partial(fock_kernel, batches, share), out_shape=...  32.4 us
    ppermute x1, starting transfers between devices, shards(): arrived = lax.ppermute(far, 'grid', route)  5.36 us
    pallas_call x1, Pallas kernels, fock_far(): pl.pallas_call(functools.partial(far_kernel, batches, share), out_shape=j...  4.1 us
  transfers between devices with their start and end apart: 1, of which 0 were waited for; matrix products, arithmetic and copies ran while one was open for 0% of the time, Pallas kernels for 21%

profile of v1, /device:TPU:9, one launch (start us, length us, event | category | flops | bytes accessed | tf_op | source)
XLA Modules:
  0.0 156.4 jit_solution(13831573920478998136)
XLA Ops:
  0.0 0.7 pad_add_fusion
  0.7 0.1 copy.11
  0.8 1.4 copy.12.mask_ref
  2.2 0.6 pad.4.meta_ref
  2.8 109.0 %potentials.1 = (bf16[6,8,256,768]{3,2,1,0:T(8,128)(2,1)}, s32[6,8,128]{2,1,0:T(8,128)}, f32[6,4,2,12,256]{4,3,2,1,0:T(8,128)}) custom-call(bf16[8,256,768]{2,1,0:T(8,128)(2,1)} %phi_ref.1, s32[8,128]{1,0:T(8,128)} %pad.4.meta_ref, bf16[2,12,32,1408]{3,2,1,0:T(8,128)(2,1)} %dens_ref.1, s32[8]{0:T(128)} %starts_ref.1, s32[8]{0:T(128)} %counts_ref.1, ...), custom_call_target="tpu_custom_call" | custom-call | flops 16999999488 | bytes 50000000 | tf_op jit(solution)/shard_map/potentials/pallas_call | solution.py:317
  111.8 0.0 copy-start
  111.8 4.1 %fock_far.1 = f32[12,32,768]{2,1,0:T(8,128)} custom-call(s32[6,8,128]{2,1,0:T(8,128)} %get-tuple-element.8.meta_ref, f32[48,12,256]{2,1,0:T(8,128)} %bitcast.9, bf16[6,8,256,768]{3,2,1,0:T(8,128)(2,1)} %get-tuple-element.10.phi_ref), custom_call_target="tpu_custom_call" | custom-call | flops 1000000000 | bytes 2000000 | tf_op jit(solution)/shard_map/fock_far/pallas_call | solution.py:501
  115.9 5.4 %collective-permute-start = (f32[12,32,768]{2,1,0:T(8,128)}, f32[12,32,768]{2,1,0:T(8,128)S(1)}, u32[]{:S(2)}, u32[]{:S(2)}) collective-permute-start(f32[12,32,768]{2,1,0:T(8,128)} %fock_far.1), channel_id=1, source_target_pairs={{0,124},{4,8},{8,4},{12,16},{16,12},{20,24},{24,20},{28,32},{32,28... | collective-permute-start | bytes 3538952 | tf_op jit(solution)/shard_map/ppermute | solution.py:524
  121.2 0.0 copy-done
  121.2 0.2 convert_reduce_fusion
  121.4 0.1 broadcast_bitcast_fusion
  121.5 32.4 %fock_own.1 = f32[2,12,32,1408]{3,2,1,0:T(8,128)} custom-call(s32[6,8,128]{2,1,0:T(8,128)} %get-tuple-element.8.meta_ref, s32[64,11]{1,0:T(8,128)} %copy.12.mask_ref, f32[48,12,256]{2,1,0:T(8,128)} %bitcast.10, bf16[6,8,256,768]{3,2,1,0:T(8,128)(2,1)} %get-tuple-element.10.phi_ref), custom_call_target="tpu_custom_call" | custom-call | flops 20000000000 | bytes 20000000 | tf_op jit(solution)/shard_map/fock_own/pallas_call | solution.py:456
  153.9 0.0 collective-permute-done
  154.0 2.4 %fusion = f32[2,12,32,1408]{3,2,1,0:T(8,128)} fusion(f32[2,12,32,1408]{3,2,1,0:T(8,128)} %fock_own.1, s32[]{:T(128)S(6)} %select_n.14, s32[]{:T(128)S(6)} %select_n.15, f32[12,32,768]{2,1,0:T(8,128)S(1)} %collective-permute-done, f32[768]{0:T(1024)S(1)} %broadcast_bitcast_fusion), kind=kLoop, calls=%fused_computation.1 | loop fusion | flops 589824 | bytes 3542024 | tf_op jit(solution)/shard_map/dynamic_update_slice | solution.py:530
Async XLA Ops:
  111.8 9.5 %copy-start = (s32[64,11]{0,1:T(8,128)S(1)}, s32[64,11]{0,1:T(8,128)}, u32[]{:S(2)}) copy-start(s32[64,11]{0,1:T(8,128)} %param.11) | copy-start | bytes 8452
  115.9 38.1 %collective-permute-start = (f32[12,32,768]{2,1,0:T(8,128)}, f32[12,32,768]{2,1,0:T(8,128)S(1)}, u32[]{:S(2)}, u32[]{:S(2)}) collective-permute-start(f32[12,32,768]{2,1,0:T(8,128)} %fock_far.1), channel_id=1, source_target_pairs={{0,124},{4,8},{8,4},{12,16},{16,12},{20,24},{24,20},{28,32},{32,28... | collective-permute-start | bytes 3538952 | tf_op jit(solution)/shard_map/ppermute | solution.py:524

commit v2 on v1

v2 whole, which is shorter than its diff:
```python
import functools

import jax
import jax.numpy as jnp
from jax import lax
from jax.experimental import pallas as pl
from jax.experimental.pallas import tpu as pltpu
from jax.sharding import PartitionSpec as P

BLOCK = 128
PERTS = 12
WINDOW = 6
POINTS = 256
REACH = 5
BAND = 11
COLS = WINDOW * BLOCK
WIDE = BAND * BLOCK
SLOTS = 6
MESH = pl.DeviceIdType.MESH
NT = (((1,), (1,)), ((), ()))


def one_hot(share, columns, first):
    rows = lax.broadcasted_iota(jnp.int32, (share, columns), 0)
    lanes = lax.broadcasted_iota(jnp.int32, (share, columns), 1)
    return jnp.where(lanes == rows + first, 1.0, 0.0).astype(jnp.bfloat16)


def density_kernel(
    chips, planes, batches, share,
    phi_ref, dens_ref, starts_ref, counts_ref, mask_ref, kern_ref,
    all_ref, meta_all_ref, pot_ref,
    phi_v, dens_v, far_v, left_v, left_far, meta_v, meta_all_v, meta_s, mask_s, part, gathered, pot_v,
    own_sem, out_sem, core_s, core_r, y_s, y_r, z_s, z_r, c_s, c_r, m_s, m_r, f_sem, a_s, a_r, b_s, b_r,
):
    grid_pos, plane = lax.axis_index("grid"), lax.axis_index("basis")
    chip, core = grid_pos // 2, lax.rem(grid_pos, 2)
    half = batches // 2
    quarter = half // 2
    per_plane = batches // planes
    own_slot = 2 + core
    far_slot = jnp.where(core == 0, 4, 1)
    first = lax.rem(plane, 2) * half
    there = half - first
    rows_all = PERTS * share
    cut = POINTS // 2

    def device(slot, at_plane):
        return (2 * lax.rem(chip + slot // 2 - 1 + chips, chips) + lax.rem(slot, 2), at_plane)

    other = (2 * chip + 1 - core, plane)

    def remote(src, dst, send, recv, to):
        return pltpu.make_async_remote_copy(
            src_ref=src, dst_ref=dst, send_sem=send, recv_sem=recv, device_id=to, device_id_type=MESH)

    def is_other(slot, at_plane):
        return jnp.logical_or(slot != own_slot, at_plane != plane)

    def for_others(act):
        @pl.loop(0, SLOTS * planes)
        def _(no):
            slot, at_plane = no // planes, lax.rem(no, planes)

            @pl.when(is_other(slot, at_plane))
            def _():
                act(slot, at_plane)

    own_copy = pltpu.make_async_copy(phi_ref, phi_v.at[own_slot], own_sem.at[0])
    own_copy.start()
    dens_copy = pltpu.make_async_copy(dens_ref, left_v, own_sem.at[1])
    dens_copy.start()
    mask_copy = pltpu.make_async_copy(mask_ref, mask_s, own_sem.at[2])
    mask_copy.start()

    line = lax.broadcasted_iota(jnp.int32, (2 * batches, BLOCK), 0)
    meta = jnp.zeros((2 * batches, BLOCK), jnp.int32)
    for no in range(batches):
        meta = jnp.where(line == no, starts_ref[no], meta)
        meta = jnp.where(line == batches + no, counts_ref[no], meta)
    meta_v[...] = meta
    meta_all_v[own_slot] = meta

    barrier = pltpu.get_barrier_semaphore()
    for slot in (0, 1, 4, 5):
        pl.semaphore_signal(barrier, inc=1, device_id=device(slot, plane), device_id_type=MESH)
    for partner in (other, (grid_pos, lax.rem(plane + 1, planes)), (grid_pos, lax.rem(plane + planes - 1, planes))):
        pl.semaphore_signal(barrier, inc=1, device_id=partner, device_id_type=MESH)
    pl.semaphore_wait(barrier, 7)

    def piece(way, n):
        return n // 2 + quarter * lax.rem(n + way, 2)

    def rows(h):
        return pl.ds(h * cut, cut)

    def y_copy(way, n, h):
        at = first + piece(way, n)
        return remote(phi_ref.at[at, rows(h)], phi_v.at[4 * way + core, at, rows(h)], y_s.at[way, n, h], y_r.at[way, n, h],
                      device(4 - 4 * way + core, plane))

    def z_copy(way, n, h):
        which = piece(way, n)
        where = phi_v.at[4 * way + core, first + which, rows(h)]
        to = lax.rem(plane + 1 - 2 * (which // quarter) + planes, planes)
        return remote(where, where, z_s.at[way, n, h], z_r.at[way, n, h], (grid_pos, to))

    def c_copy(way, m, h):
        at = jnp.where(m < half, first, there) + piece(way, lax.rem(m, half))
        where = phi_v.at[4 * way + core, at, rows(h)]
        return remote(where, where, c_s.at[way, m, h], c_r.at[way, m, h], other)

    def core_copy(no):
        return remote(phi_ref.at[no], phi_v.at[own_slot, no], core_s.at[no], core_r.at[no], other)

    def meta_copy(way, s):
        return remote(meta_v, meta_all_v.at[4 * way + core], m_s.at[1 + 2 * way + s], m_r.at[1 + 2 * way + core],
                      device(4 - 4 * way + s, plane))

    def out_copy(slot, no):
        return pltpu.make_async_copy(phi_v.at[slot, no], all_ref.at[slot, no], out_sem.at[slot, no])

    far_copy = remote(dens_ref.at[core, :, :, pl.ds(pl.multiple_of(core * REACH * BLOCK, BLOCK), COLS)], left_far,
                      f_sem.at[0], f_sem.at[1], device(jnp.where(core == 0, 1, 4), plane))
    core_meta = remote(meta_v, meta_all_v.at[own_slot], m_s.at[0], m_r.at[0], other)

    core_meta.start()
    for way in range(2):
        for s in range(2):
            meta_copy(way, s).start()

    @pl.loop(0, half)
    def _(n):
        for h in range(2):
            for way in range(2):
                y_copy(way, n, h).start()

    far_copy.start()

    @pl.loop(0, batches)
    def _(no):
        core_copy(no).start()

    def masked(block, keep):
        return block * keep.astype(jnp.float32).astype(block.dtype)

    def same(left, right):
        return (1 - jnp.minimum(jnp.abs(left - right), 1)).astype(jnp.float32)

    mask_copy.wait()
    dens_copy.wait()
    for r in range(2):
        row = 2 * grid_pos + r
        for t in range(BAND):
            block = left_v[r, :, :, t * BLOCK:(t + 1) * BLOCK].reshape(rows_all, BLOCK)
            dens_v[r, t, :rows_all, :] = masked(block, mask_s[row, t])
            dens_v[r, t, rows_all:, :] = one_hot(share, BLOCK, (REACH - t) * BLOCK + plane * share)
    far_v[rows_all:, :] = one_hot(share, COLS, core * REACH * BLOCK + plane * share)

    own_copy.wait()
    for no in range(5):
        pltpu.make_async_copy(meta_v, meta_all_v.at[own_slot], m_r.at[no]).wait()
    to_smem = pltpu.make_async_copy(meta_all_v, meta_s, own_sem.at[3])
    to_smem.start()
    meta_out = pltpu.make_async_copy(meta_all_v, meta_all_ref, own_sem.at[4])
    meta_out.start()
    to_smem.wait()

    def reduced(mixed):
        picked = mixed[rows_all:rows_all + share]
        sums = jnp.sum(mixed[:rows_all].reshape(PERTS, share, POINTS) * picked[None], axis=1)
        return jnp.concatenate([sums[:, :cut], sums[:, cut:]], axis=0)

    def rho_part(slot, no):
        start = meta_s[slot, no, 0]
        phi = phi_v[slot, no]
        total = None
        for r in range(2):
            offset = 2 * grid_pos + r - start
            inside = jnp.clip(offset, 0, WINDOW - 1)
            lhs = jnp.concatenate([dens_v[r, REACH - inside + c] for c in range(WINDOW)], axis=1)
            mixed = lax.dot_general(lhs, phi, NT, preferred_element_type=jnp.float32)
            term = reduced(mixed) * same(offset, inside)
            total = term if total is None else total + term
        part[slot, no] = total

    far_start = 4 * chip - 1

    def rho_far(slot, no):
        mixed = lax.dot_general(far_v[...], phi_v[slot, no], NT, preferred_element_type=jnp.float32)
        part[slot, no] = part[slot, no] + reduced(mixed) * same(meta_s[slot, no, 0], far_start)

    def part_copy(slot, no):
        back = 2 * (2 - slot // 2) + core
        keeper = no // per_plane
        which = lax.rem(no, per_plane)
        return remote(part.at[slot, no], gathered.at[back, plane, which], a_s.at[slot, no], a_r.at[back, plane, which],
                      device(slot, keeper))

    def send_part(slot, no):
        away = is_other(slot, no // per_plane)

        @pl.when(away)
        def _():
            part_copy(slot, no).start()

        @pl.when(jnp.logical_not(away))
        def _():
            gathered[own_slot, plane, lax.rem(no, per_plane)] = part[slot, no]

    def items(n, act):
        @pl.loop(0, 8)
        def _(item):
            kind, way = item // 2, lax.rem(item, 2)
            late = jnp.where(kind == 0, 0, jnp.where(kind == 3, 2, 1))
            came = n - late
            slot = 4 * way + jnp.where(kind <= 1, core, 1 - core)
            at = jnp.where(lax.rem(kind, 2) == 0, first, there) + piece(way, jnp.maximum(came, 0))

            @pl.when(jnp.logical_and(came >= 0, came < half))
            def _():
                act(slot, at)

    def send_near(slot, no):
        @pl.when(slot != far_slot)
        def _():
            send_part(slot, no)

    @pl.loop(0, batches)
    def _(no):
        out_copy(own_slot, no).start()
        rho_part(own_slot, no)

    @pl.loop(0, half + 2)
    def _(n):
        @pl.when(n < half)
        def _():
            for h in range(2):
                for way in range(2):
                    y_copy(way, n, h).wait_recv()
                    z_copy(way, n, h).start()
                    c_copy(way, n, h).start()
            for way in range(2):
                out_copy(4 * way + core, first + piece(way, n)).start()

        @pl.when(jnp.logical_and(n >= 1, n <= half))
        def _():
            for h in range(2):
                for way in range(2):
                    z_copy(way, n - 1, h).wait_recv()
                    c_copy(way, half + n - 1, h).start()
            for way in range(2):
                out_copy(4 * way + core, there + piece(way, n - 1)).start()
            for way in range(2):
                for h in range(2):
                    c_copy(way, n - 1, h).wait_recv()
                out_copy(4 * way + 1 - core, first + piece(way, n - 1)).start()

        @pl.when(n >= 2)
        def _():
            for way in range(2):
                for h in range(2):
                    c_copy(way, half + n - 2, h).wait_recv()
                out_copy(4 * way + 1 - core, there + piece(way, n - 2)).start()

        @pl.when(n == half)
        def _():
            @pl.loop(0, batches)
            def _(no):
                for slot in range(2):
                    send_part(2 + slot, no)

            @pl.loop(0, half)
            def _(m):
                items(m, send_near)

        items(n, rho_part)

        @pl.when(n >= half)
        def _():
            items(n, send_near)

        @pl.when(n == 0)
        def _():
            @pl.loop(0, batches)
            def _(no):
                core_copy(no).wait_recv()
                out_copy(5 - own_slot, no).start()
                rho_part(5 - own_slot, no)

        @pl.when(n == half)
        def _():
            far_copy.wait_recv()
            far_row = jnp.where(core == 0, jnp.maximum(2 * grid_pos - 1, 0), jnp.minimum(2 * grid_pos + 2, 4 * chips - 1))
            for t in range(WINDOW):
                block = left_far[:, :, t * BLOCK:(t + 1) * BLOCK].reshape(rows_all, BLOCK)
                keep = mask_s[far_row, jnp.where(core == 0, REACH, 0) + t]
                far_v[:rows_all, t * BLOCK:(t + 1) * BLOCK] = masked(block, keep)

            @pl.loop(0, batches)
            def _(no):
                rho_far(far_slot, no)
                send_part(far_slot, no)

    def pot_copy(slot, at_plane):
        back = 2 * (2 - slot // 2) + core
        return remote(pot_v, pot_ref.at[back, plane], b_s.at[slot, at_plane], b_r.at[back, plane],
                      device(slot, at_plane))

    def wait_parts(slot, at_plane):
        for which in range(per_plane):
            pltpu.make_async_copy(part.at[0, 0], gathered.at[slot, at_plane, which], a_r.at[slot, at_plane, which]).wait()

    for_others(wait_parts)
    points = lax.broadcasted_iota(jnp.int32, (1, POINTS), 1)
    for no in range(per_plane):
        rho = gathered[0, 0, no]
        for slot in range(SLOTS):
            for at_plane in range(planes):
                if slot or at_plane:
                    rho = rho + gathered[slot, at_plane, no]
        mine = per_plane * plane + no
        live = jnp.clip(counts_ref[mine] - points, 0, 1).astype(jnp.float32)
        factor = jnp.broadcast_to(kern_ref[pl.ds(mine, 1), :] * live, (PERTS, POINTS))
        pot_v[no] = rho * jnp.concatenate([factor[:, :cut], factor[:, cut:]], axis=0)
    for_others(lambda slot, at_plane: pot_copy(slot, at_plane).start())
    pot_own = pltpu.make_async_copy(pot_v, pot_ref.at[own_slot, plane], own_sem.at[0])
    pot_own.start()

    meta_out.wait()
    far_copy.wait_send()
    core_meta.wait_send()
    for way in range(2):
        for s in range(2):
            meta_copy(way, s).wait_send()

    @pl.loop(0, batches)
    def _(no):
        core_copy(no).wait_send()
        for slot in range(SLOTS):
            out_copy(slot, no).wait()

            @pl.when(is_other(slot, no // per_plane))
            def _():
                part_copy(slot, no).wait_send()

    @pl.loop(0, half)
    def _(n):
        for h in range(2):
            for way in range(2):
                y_copy(way, n, h).wait_send()
                z_copy(way, n, h).wait_send()
                c_copy(way, n, h).wait_send()
                c_copy(way, half + n, h).wait_send()

    for_others(lambda slot, at_plane: pltpu.make_async_copy(
        pot_v, pot_ref.at[slot, at_plane], b_r.at[slot, at_plane]).wait())
    pot_own.wait()
    for_others(lambda slot, at_plane: pot_copy(slot, at_plane).wait_send())


def potentials(phi, density, starts, counts, pair_mask, kern, chips, planes):
    batches, points, cols = phi.shape
    share = density.shape[2]
    half, per_plane = batches // 2, batches // planes
    rows = PERTS * share + share
    far = pl.BlockSpec(memory_space=pl.ANY)
    smem = pl.BlockSpec(memory_space=pltpu.SMEM)
    vmem = pl.BlockSpec(memory_space=pltpu.VMEM)
    dma = pltpu.SemaphoreType.DMA
    f32 = jnp.float32
    row_pair = (2 * PERTS, points // 2)
    meta = (2 * batches, BLOCK)
    return pl.pallas_call(
        functools.partial(density_kernel, chips, planes, batches, share),
        out_shape=(
            jax.ShapeDtypeStruct((SLOTS, batches, points, cols), phi.dtype),
            jax.ShapeDtypeStruct((SLOTS,) + meta, starts.dtype),
            jax.ShapeDtypeStruct((SLOTS, planes, per_plane) + row_pair, f32),
        ),
        in_specs=[far, far, smem, smem, far, vmem],
        out_specs=[far] * 3,
        scratch_shapes=[
            pltpu.VMEM((SLOTS, batches, points, cols), phi.dtype),
            pltpu.VMEM((2, BAND, rows, BLOCK), density.dtype),
            pltpu.VMEM((rows, COLS), density.dtype),
            pltpu.VMEM(density.shape, density.dtype),
            pltpu.VMEM((PERTS, share, COLS), density.dtype),
            pltpu.VMEM(meta, starts.dtype),
            pltpu.VMEM((SLOTS,) + meta, starts.dtype),
            pltpu.SMEM((SLOTS,) + meta, starts.dtype),
            pltpu.SMEM(pair_mask.shape, pair_mask.dtype),
            pltpu.VMEM((SLOTS, batches) + row_pair, f32),
            pltpu.VMEM((SLOTS, planes, per_plane) + row_pair, f32),
            pltpu.VMEM((per_plane,) + row_pair, f32),
            dma((5,)), dma((SLOTS, batches)), dma((batches,)), dma((batches,)),
            dma((2, half, 2)), dma((2, half, 2)), dma((2, half, 2)), dma((2, half, 2)),
            dma((2, batches, 2)), dma((2, batches, 2)), dma((5,)), dma((5,)), dma((2,)),
            dma((SLOTS, batches)), dma((SLOTS, planes, per_plane)), dma((SLOTS, planes)), dma((SLOTS, planes)),
        ],
        compiler_params=pltpu.CompilerParams(collective_id=0, has_side_effects=True, vmem_limit_bytes=56 << 20),
        cost_estimate=pl.CostEstimate(flops=17 * 10**9, bytes_accessed=50 * 10**6, transcendentals=0),
        name="potentials",
    )(phi, density, starts, counts, pair_mask, kern)


def joined(halves):
    return jnp.concatenate([halves[:PERTS], halves[PERTS:]], axis=1)


def split_weights(pot, picked, share):
    weighted = (pot[:, None, :] * picked[None]).reshape(PERTS * share, POINTS)
    high = weighted.astype(jnp.bfloat16)
    low = (weighted - high.astype(jnp.float32)).astype(jnp.bfloat16)
    return high, low


def add_product(parts, phi, few, store):
    def product(points):
        left = jnp.concatenate(
            [jnp.concatenate([high[:, :points], low[:, :points]], axis=1) for high, low in parts], axis=0)
        right = phi[:points, :]
        store(jnp.dot(left, jnp.concatenate([right, right], axis=0), preferred_element_type=jnp.float32))

    @pl.when(few)
    def _():
        product(POINTS // 2)

    @pl.when(jnp.logical_not(few))
    def _():
        product(POINTS)


DEPTH = 4


def fock_kernel(batches, share, meta_ref, mask_ref, pot_ref, phi_ref, out_ref, chosen, buf, sems):
    grid_pos, plane = lax.axis_index("grid"), lax.axis_index("basis")
    base = 2 * grid_pos - REACH

    def note(no, count):
        lead = meta_ref[no // batches, lax.rem(no, batches), 0] - base
        near = jnp.logical_and(lead >= 0, lead <= REACH + 1)

        @pl.when(near)
        def _():
            chosen[count] = no

        return count + near.astype(jnp.int32)

    count = lax.fori_loop(0, SLOTS * batches, note, 0)

    def fetch(i):
        no = chosen[i]
        return pltpu.make_async_copy(
            phi_ref.at[no // batches, lax.rem(no, batches)], buf.at[lax.rem(i, DEPTH)], sems.at[lax.rem(i, DEPTH)])

    for i in range(DEPTH - 1):
        @pl.when(i < count)
        def _():
            fetch(i).start()

    out_ref[...] = jnp.zeros_like(out_ref)
    pick = one_hot(share, BLOCK, plane * share)

    @pl.loop(0, count)
    def _(i):
        fetch(i).wait()

        @pl.when(i + DEPTH - 1 < count)
        def _():
            fetch(i + DEPTH - 1).start()

        no = chosen[i]
        lead = meta_ref[no // batches, lax.rem(no, batches), 0] - base
        few = meta_ref[no // batches, batches + lax.rem(no, batches), 0] <= POINTS // 2
        here = buf.at[lax.rem(i, DEPTH)]
        pot = joined(pot_ref[no])

        def weights(offset):
            own = here[:, pl.ds(pl.multiple_of(offset * BLOCK, BLOCK), BLOCK)]
            picked = lax.dot_general(pick, own, NT, preferred_element_type=jnp.float32)
            return split_weights(pot, picked, share)

        def add(r, offset, value):
            spot = out_ref.at[r, :, :, pl.ds(pl.multiple_of((REACH - offset) * BLOCK, BLOCK), COLS)]
            spot[...] = spot[...] + value.reshape(PERTS, share, COLS)

        both = jnp.logical_and(lead >= 1, lead <= REACH)

        @pl.when(both)
        def _():
            offset = REACH - lead
            parts = [weights(offset), weights(offset + 1)]
            rows = PERTS * share

            def store(value):
                add(0, offset, value[:rows])
                add(1, offset + 1, value[rows:])

            add_product(parts, here, few, store)

        @pl.when(jnp.logical_not(both))
        def _():
            r = jnp.where(lead == 0, 0, 1)
            offset = jnp.where(lead == 0, REACH, 0)
            add_product([weights(offset)], here, few, lambda value: add(r, offset, value))

    for r in range(2):
        for t in range(BAND):
            @pl.when(mask_ref[2 * grid_pos + r, t] == 0)
            def _():
                out_ref[r, :, :, t * BLOCK:(t + 1) * BLOCK] = jnp.zeros((PERTS, share, BLOCK), jnp.float32)


def fock_own(meta_all, pair_mask, pot, phi_all, share):
    slots, batches, points, cols = phi_all.shape
    smem = pl.BlockSpec(memory_space=pltpu.SMEM)
    vmem = pl.BlockSpec(memory_space=pltpu.VMEM)
    return pl.pallas_call(
        functools.partial(fock_kernel, batches, share),
        out_shape=jax.ShapeDtypeStruct((2, PERTS, share, WIDE), jnp.float32),
        in_specs=[smem, smem, vmem, pl.BlockSpec(memory_space=pl.ANY)],
        out_specs=vmem,
        scratch_shapes=[
            pltpu.SMEM((slots * batches,), jnp.int32),
            pltpu.VMEM((DEPTH, points, cols), phi_all.dtype),
            pltpu.SemaphoreType.DMA((DEPTH,)),
        ],
        compiler_params=pltpu.CompilerParams(vmem_limit_bytes=56 << 20),
        cost_estimate=pl.CostEstimate(flops=20 * 10**9, bytes_accessed=20 * 10**6, transcendentals=0),
        name="fock_own",
    )(meta_all, pair_mask, pot, phi_all)


def far_kernel(batches, share, meta_ref, pot_ref, phi_ref, out_ref, buf, sem):
    grid_pos, plane = lax.axis_index("grid"), lax.axis_index("basis")
    core = lax.rem(grid_pos, 2)
    slot = jnp.where(core == 0, 4, 1)
    far_start = 4 * (grid_pos // 2) - 1
    out_ref[...] = jnp.zeros_like(out_ref)
    pick = one_hot(share, BLOCK, plane * share)

    @pl.loop(0, batches)
    def _(no):
        @pl.when(meta_ref[slot, no, 0] == far_start)
        def _():
            copy = pltpu.make_async_copy(phi_ref.at[slot, no], buf, sem)
            copy.start()
            copy.wait()
            own = buf[:, pl.ds(pl.multiple_of(core * REACH * BLOCK, BLOCK), BLOCK)]
            picked = lax.dot_general(pick, own, NT, preferred_element_type=jnp.float32)
            parts = [split_weights(joined(pot_ref[slot * batches + no]), picked, share)]

            def store(value):
                out_ref[...] += value.reshape(PERTS, share, COLS)

            add_product(parts, buf, meta_ref[slot, batches + no, 0] <= POINTS // 2, store)


def fock_far(meta_all, pot, phi_all, share):
    slots, batches, points, cols = phi_all.shape
    smem = pl.BlockSpec(memory_space=pltpu.SMEM)
    vmem = pl.BlockSpec(memory_space=pltpu.VMEM)
    return pl.pallas_call(
        functools.partial(far_kernel, batches, share),
        out_shape=jax.ShapeDtypeStruct((PERTS, share, COLS), jnp.float32),
        in_specs=[smem, vmem, pl.BlockSpec(memory_space=pl.ANY)],
        out_specs=vmem,
        scratch_shapes=[pltpu.VMEM((points, cols), phi_all.dtype), pltpu.SemaphoreType.DMA],
        compiler_params=pltpu.CompilerParams(vmem_limit_bytes=56 << 20),
        cost_estimate=pl.CostEstimate(flops=10**9, bytes_accessed=2 * 10**6, transcendentals=0),
        name="fock_far",
    )(meta_all, pot, phi_all)


def shards(density, basis_vals, kernel, starts, counts, pair_mask):
    grid_size, planes = lax.axis_size("grid"), lax.axis_size("basis")
    batches, share = basis_vals.shape[0], density.shape[2]
    grid_pos = lax.axis_index("grid")
    core = lax.rem(grid_pos, 2)
    phi_all, meta_all, pot = potentials(
        basis_vals, density, starts, counts, pair_mask, kernel, grid_size // 2, planes)
    pot = pot.reshape(SLOTS * batches, 2 * PERTS, POINTS // 2)
    far = fock_far(meta_all, pot, phi_all, share)
    route = [(i, (i + 1) % grid_size if i % 2 else (i - 1) % grid_size) for i in range(grid_size)]
    arrived = lax.ppermute(far, "grid", route)
    own = fock_own(meta_all, pair_mask, pot, phi_all, share)
    mask_row = lax.dynamic_slice(pair_mask, (2 * grid_pos + core, core * REACH), (1, WINDOW))[0]
    keep = jnp.repeat(mask_row, BLOCK).astype(jnp.float32)
    place = (core, 0, 0, core * REACH * BLOCK)
    present = lax.dynamic_slice(own, place, (1, PERTS, share, COLS))
    return lax.dynamic_update_slice(own, present + (arrived * keep)[None], place)


def solution(mesh):
    placed = (
        P("grid", None, "basis", None),
        P("grid", None, None),
        P("grid", None),
        P("grid"),
        P("grid"),
        P(),
    )
    return jax.shard_map(
        shards,
        mesh=mesh,
        in_specs=placed,
        out_specs=P("grid", None, "basis", None),
        check_vma=False,
    )
```

time: 158 us -> 128 us (0.81)
  Pallas kernels: 146 us -> 123 us
  starting transfers between devices: 5.36 us -> 0.08 us
    pallas_call x1, Pallas kernels: 109 us -> 82 us  [potentials(): pl.pallas_call(functools.partial(density_kernel, chips, planes, batches,...]
    ppermute x1, starting transfers between devices: 5.36 us -> 0.08 us  [shards(): arrived = lax.ppermute(far, 'grid', route)]
    pallas_call x1, Pallas kernels: 4.1 us -> 9.2 us  [fock_far(): pl.pallas_call(functools.partial(far_kernel, batches, share), out_shape=j...]
  transfers between devices with their start and end apart: 1 -> 1, of which waited for: 0 -> 0; matrix products, arithmetic and copies ran while one was open for 0% -> 0% of each run, Pallas kernels for 21% -> 25%
where the time goes in v2:
time: 128 us; the launch traced here: 127 us
  Pallas kernels  123 us (96%)
  other arithmetic  2.62 us (2%)
  local copies, waits for them, and re-layouts  1.46 us (1%)
    pallas_call x1, Pallas kernels, potentials(): pl.pallas_call(functools.partial(density_kernel, chips, planes, batches,...  82 us
    pallas_call x1, Pallas kernels, fock_own(): pl.pallas_call(functools.partial(fock_kernel, batches, share), out_shape=...  31.9 us
    pallas_call x1, Pallas kernels, fock_far(): pl.pallas_call(functools.partial(far_kernel, batches, share), out_shape=j...  9.2 us
  transfers between devices with their start and end apart: 1, of which 0 were waited for; matrix products, arithmetic and copies ran while one was open for 0% of the time, Pallas kernels for 25%

profile of v2, /device:TPU:9, one launch (start us, length us, event | category | flops | bytes accessed | tf_op | source)
XLA Modules:
  0.0 127.3 jit_solution(6978833982892473937)
XLA Ops:
  0.0 1.4 %copy.7.mask_ref = s32[64,11]{1,0:T(8,128)} copy(s32[64,11]{0,1:T(8,128)} %param.11) | data formatting | bytes 5632 | tf_op args[5]
  1.4 82.0 %potentials.1 = (bf16[6,8,256,768]{3,2,1,0:T(8,128)(2,1)}, s32[6,16,128]{2,1,0:T(8,128)}, f32[6,4,2,24,128]{4,3,2,1,0:T(8,128)}) custom-call(bf16[8,256,768]{2,1,0:T(8,128)(2,1)} %phi_ref.1, bf16[2,12,32,1408]{3,2,1,0:T(8,128)(2,1)} %dens_ref.1, s32[8]{0:T(128)} %starts_ref.1, s32[8]{0:T(128)} %counts_ref.1, s32[64,11]{1,0:T(8,128)} %copy.7.mask_ref, ...), custom_call_target="tpu_custom_call" | custom-call | flops 16999999488 | bytes 50000000 | tf_op jit(solution)/shard_map/potentials/pallas_call | solution.py:374
  83.3 0.0 copy-start
  83.4 9.2 %fock_far.1 = f32[12,32,768]{2,1,0:T(8,128)} custom-call(s32[6,16,128]{2,1,0:T(8,128)} %get-tuple-element.8.meta_ref, f32[48,24,128]{2,1,0:T(8,128)} %bitcast.7, bf16[6,8,256,768]{3,2,1,0:T(8,128)(2,1)} %get-tuple-element.10.phi_ref), custom_call_target="tpu_custom_call" | custom-call | flops 1000000000 | bytes 2000000 | tf_op jit(solution)/shard_map/fock_far/pallas_call | solution.py:565
  92.6 0.1 collective-permute-start
  92.7 0.0 copy-done
  92.7 0.2 convert_reduce_fusion
  92.9 0.1 broadcast_bitcast_fusion
  93.0 31.9 %fock_own.1 = f32[2,12,32,1408]{3,2,1,0:T(8,128)} custom-call(s32[6,16,128]{2,1,0:T(8,128)} %get-tuple-element.8.meta_ref, s32[64,11]{1,0:T(8,128)} %copy.7.mask_ref, f32[48,24,128]{2,1,0:T(8,128)} %bitcast.8, bf16[6,8,256,768]{3,2,1,0:T(8,128)(2,1)} %get-tuple-element.10.phi_ref), custom_call_target="tpu_custom_call" | custom-call | flops 20000000000 | bytes 20000000 | tf_op jit(solution)/shard_map/fock_own/pallas_call | solution.py:520
  124.8 0.0 collective-permute-done
  124.8 2.4 %fusion = f32[2,12,32,1408]{3,2,1,0:T(8,128)} fusion(f32[2,12,32,1408]{3,2,1,0:T(8,128)} %fock_own.1, s32[]{:T(128)S(6)} %select_n.14, s32[]{:T(128)S(6)} %select_n.15, f32[12,32,768]{2,1,0:T(8,128)S(1)} %collective-permute-done, f32[768]{0:T(1024)S(1)} %broadcast_bitcast_fusion), kind=kLoop, calls=%fused_computation.1 | loop fusion | flops 589824 | bytes 3542024 | tf_op jit(solution)/shard_map/dynamic_update_slice | solution.py:593
Async XLA Ops:
  83.3 9.3 %copy-start = (s32[64,11]{0,1:T(8,128)S(1)}, s32[64,11]{0,1:T(8,128)}, u32[]{:S(2)}) copy-start(s32[64,11]{0,1:T(8,128)} %param.11) | copy-start | bytes 8452
  92.6 32.3 %collective-permute-start = (f32[12,32,768]{2,1,0:T(8,128)}, f32[12,32,768]{2,1,0:T(8,128)S(1)}, u32[]{:S(2)}, u32[]{:S(2)}) collective-permute-start(f32[12,32,768]{2,1,0:T(8,128)} %fock_far.1), channel_id=1, source_target_pairs={{0,124},{4,8},{8,4},{12,16},{16,12},{20,24},{24,20},{28,32},{32,28... | collective-permute-start | bytes 3538952 | tf_op jit(solution)/shard_map/ppermute | solution.py:587

commit v3 on v2

--- a/solution.py
+++ b/solution.py
@@ -29,8 +29,8 @@
 def density_kernel(
     chips, planes, batches, share,
     phi_ref, dens_ref, starts_ref, counts_ref, mask_ref, kern_ref,
-    all_ref, meta_all_ref, pot_ref,
-    phi_v, dens_v, far_v, left_v, left_far, meta_v, meta_all_v, meta_s, mask_s, part, gathered, pot_v,
+    all_ref, facts_ref, pot_ref, picks_ref, far_picks_ref,
+    phi_v, dens_v, far_v, left_v, left_far, meta_v, meta_all_v, facts_v, meta_s, mask_s, picks_v, far_picks_v, part, gathered, pot_v,
     own_sem, out_sem, core_s, core_r, y_s, y_r, z_s, z_r, c_s, c_r, m_s, m_r, f_sem, a_s, a_r, b_s, b_r,
 ):
     grid_pos, plane = lax.axis_index("grid"), lax.axis_index("basis")
@@ -73,11 +73,12 @@
     mask_copy = pltpu.make_async_copy(mask_ref, mask_s, own_sem.at[2])
     mask_copy.start()
 
-    line = lax.broadcasted_iota(jnp.int32, (2 * batches, BLOCK), 0)
-    meta = jnp.zeros((2 * batches, BLOCK), jnp.int32)
+    line = lax.broadcasted_iota(jnp.int32, (8, BLOCK), 0)
+    lane = lax.broadcasted_iota(jnp.int32, (8, BLOCK), 1)
+    meta = jnp.zeros((8, BLOCK), jnp.int32)
     for no in range(batches):
-        meta = jnp.where(line == no, starts_ref[no], meta)
-        meta = jnp.where(line == batches + no, counts_ref[no], meta)
+        meta = jnp.where(lane == no, starts_ref[no], meta)
+        meta = jnp.where(lane == batches + no, counts_ref[no], meta)
     meta_v[...] = meta
     meta_all_v[own_slot] = meta
 
@@ -160,27 +161,41 @@
     own_copy.wait()
     for no in range(5):
         pltpu.make_async_copy(meta_v, meta_all_v.at[own_slot], m_r.at[no]).wait()
-    to_smem = pltpu.make_async_copy(meta_all_v, meta_s, own_sem.at[3])
+    facts = jnp.zeros((8, BLOCK), jnp.int32)
+    for slot in range(SLOTS):
+        facts = jnp.where(line == slot, meta_all_v[slot], facts)
+    for r in range(2):
+        for t in range(BAND):
+            facts = jnp.where(jnp.logical_and(line == SLOTS + r, lane == t), mask_s[2 * grid_pos + r, t], facts)
+    facts_v[...] = facts
+    to_smem = pltpu.make_async_copy(facts_v, meta_s, own_sem.at[3])
     to_smem.start()
-    meta_out = pltpu.make_async_copy(meta_all_v, meta_all_ref, own_sem.at[4])
-    meta_out.start()
+    facts_out = pltpu.make_async_copy(facts_v, facts_ref, own_sem.at[4])
+    facts_out.start()
     to_smem.wait()
 
-    def reduced(mixed):
-        picked = mixed[rows_all:rows_all + share]
+    def reduced(mixed, keep_picks):
+        picked = mixed[rows_all:]
+        for h in range(2):
+            keep_picks(h, picked[:, h * cut:(h + 1) * cut].astype(jnp.bfloat16))
         sums = jnp.sum(mixed[:rows_all].reshape(PERTS, share, POINTS) * picked[None], axis=1)
         return jnp.concatenate([sums[:, :cut], sums[:, cut:]], axis=0)
 
     def rho_part(slot, no):
-        start = meta_s[slot, no, 0]
-        phi = phi_v[slot, no]
-        total = None
+        start = meta_s[slot, no]
+        lhs, keeps = [], []
         for r in range(2):
             offset = 2 * grid_pos + r - start
             inside = jnp.clip(offset, 0, WINDOW - 1)
-            lhs = jnp.concatenate([dens_v[r, REACH - inside + c] for c in range(WINDOW)], axis=1)
-            mixed = lax.dot_general(lhs, phi, NT, preferred_element_type=jnp.float32)
-            term = reduced(mixed) * same(offset, inside)
+            keeps.append(same(offset, inside))
+            lhs.append(jnp.concatenate([dens_v[r, REACH - inside + c] for c in range(WINDOW)], axis=1))
+        mixed = lax.dot_general(jnp.concatenate(lhs, axis=0), phi_v[slot, no], NT, preferred_element_type=jnp.float32)
+        total = None
+        for r in range(2):
+            def keep_picks(h, value, r=r):
+                picks_v[slot, no, h, r] = value
+
+            term = reduced(mixed[r * (rows_all + share):(r + 1) * (rows_all + share)], keep_picks) * keeps[r]
             total = term if total is None else total + term
         part[slot, no] = total
 
@@ -188,7 +203,11 @@
 
     def rho_far(slot, no):
         mixed = lax.dot_general(far_v[...], phi_v[slot, no], NT, preferred_element_type=jnp.float32)
-        part[slot, no] = part[slot, no] + reduced(mixed) * same(meta_s[slot, no, 0], far_start)
+
+        def keep_picks(h, value):
+            far_picks_v[no, h] = value
+
+        part[slot, no] = part[slot, no] + reduced(mixed, keep_picks) * same(meta_s[slot, no], far_start)
 
     def part_copy(slot, no):
         back = 2 * (2 - slot // 2) + core
@@ -301,6 +320,11 @@
             def _(no):
                 rho_far(far_slot, no)
                 send_part(far_slot, no)
+
+    picks_out = pltpu.make_async_copy(picks_v, picks_ref, own_sem.at[1])
+    picks_out.start()
+    far_picks_out = pltpu.make_async_copy(far_picks_v, far_picks_ref, own_sem.at[2])
+    far_picks_out.start()
 
     def pot_copy(slot, at_plane):
         back = 2 * (2 - slot // 2) + core
@@ -327,7 +351,9 @@
     pot_own = pltpu.make_async_copy(pot_v, pot_ref.at[own_slot, plane], own_sem.at[0])
     pot_own.start()
 
-    meta_out.wait()
+    facts_out.wait()
+    picks_out.wait()
+    far_picks_out.wait()
     far_copy.wait_send()
     core_meta.wait_send()
     for way in range(2):
@@ -370,16 +396,19 @@
     dma = pltpu.SemaphoreType.DMA
     f32 = jnp.float32
     row_pair = (2 * PERTS, points // 2)
-    meta = (2 * batches, BLOCK)
+    meta = (8, BLOCK)
+    picks, far_picks = (SLOTS, batches, 2, 2, share, points // 2), (batches, 2, share, points // 2)
     return pl.pallas_call(
         functools.partial(density_kernel, chips, planes, batches, share),
         out_shape=(
             jax.ShapeDtypeStruct((SLOTS, batches, points, cols), phi.dtype),
-            jax.ShapeDtypeStruct((SLOTS,) + meta, starts.dtype),
+            jax.ShapeDtypeStruct(meta, starts.dtype),
             jax.ShapeDtypeStruct((SLOTS, planes, per_plane) + row_pair, f32),
+            jax.ShapeDtypeStruct(picks, phi.dtype),
+            jax.ShapeDtypeStruct(far_picks, phi.dtype),
         ),
         in_specs=[far, far, smem, smem, far, vmem],
-        out_specs=[far] * 3,
+        out_specs=[far] * 5,
         scratch_shapes=[
             pltpu.VMEM((SLOTS, batches, points, cols), phi.dtype),
             pltpu.VMEM((2, BAND, rows, BLOCK), density.dtype),
@@ -388,8 +417,11 @@
             pltpu.VMEM((PERTS, share, COLS), density.dtype),
             pltpu.VMEM(meta, starts.dtype),
             pltpu.VMEM((SLOTS,) + meta, starts.dtype),
-            pltpu.SMEM((SLOTS,) + meta, starts.dtype),
+            pltpu.VMEM(meta, starts.dtype),
+            pltpu.SMEM(meta, starts.dtype),
             pltpu.SMEM(pair_mask.shape, pair_mask.dtype),
+            pltpu.VMEM(picks, phi.dtype),
+            pltpu.VMEM(far_picks, phi.dtype),
             pltpu.VMEM((SLOTS, batches) + row_pair, f32),
             pltpu.VMEM((SLOTS, planes, per_plane) + row_pair, f32),
             pltpu.VMEM((per_plane,) + row_pair, f32),
@@ -408,170 +440,216 @@
     return jnp.concatenate([halves[:PERTS], halves[PERTS:]], axis=1)
 
 
-def split_weights(pot, picked, share):
-    weighted = (pot[:, None, :] * picked[None]).reshape(PERTS * share, POINTS)
+def split_weights(pot, picked):
+    weighted = (pot[:, None, :] * picked[None]).reshape(pot.shape[0] * picked.shape[0], picked.shape[1])
     high = weighted.astype(jnp.bfloat16)
     low = (weighted - high.astype(jnp.float32)).astype(jnp.bfloat16)
     return high, low
 
 
-def add_product(parts, phi, few, store):
-    def product(points):
-        left = jnp.concatenate(
-            [jnp.concatenate([high[:, :points], low[:, :points]], axis=1) for high, low in parts], axis=0)
-        right = phi[:points, :]
-        store(jnp.dot(left, jnp.concatenate([right, right], axis=0), preferred_element_type=jnp.float32))
-
-    @pl.when(few)
-    def _():
-        product(POINTS // 2)
-
-    @pl.when(jnp.logical_not(few))
-    def _():
-        product(POINTS)
-
-
-DEPTH = 4
-
-
-def fock_kernel(batches, share, meta_ref, mask_ref, pot_ref, phi_ref, out_ref, chosen, buf, sems):
-    grid_pos, plane = lax.axis_index("grid"), lax.axis_index("basis")
+CUT = POINTS // 2
+LARGEST = 4
+
+
+class Chunks:
+    def __init__(self, batches, facts_ref, pot, pick, phi_ref, listed, counted, buf, sems):
+        self.batches, self.facts, self.pot, self.pick, self.phi = batches, facts_ref, pot, pick, phi_ref
+        self.listed, self.counted, self.buf, self.sems = listed, counted, buf, sems
+
+    def start(self, no):
+        return self.facts[no // self.batches, lax.rem(no, self.batches)]
+
+    def note(self, which, no, wanted):
+        most = self.pot.shape[0] * 2
+        many = self.facts[no // self.batches, self.batches + lax.rem(no, self.batches)] > CUT
+
+        @pl.when(wanted)
+        def _():
+            have = self.counted[which]
+            self.listed[which * most + have] = 2 * no
+            self.listed[which * most + have + 1] = 2 * no + 1
+            self.counted[which] = have + 1 + many.astype(jnp.int32)
+
+    def copy(self, chunk):
+        no, h = chunk // 2, lax.rem(chunk, 2)
+        return pltpu.make_async_copy(
+            self.phi.at[no // self.batches, lax.rem(no, self.batches), pl.ds(pl.multiple_of(h * CUT, CUT), CUT)],
+            self.buf.at[chunk], self.sems.at[chunk])
+
+    def fetch(self, which):
+        @pl.loop(0, self.counted[which])
+        def _(i):
+            self.copy(self.listed[which * self.pot.shape[0] * 2 + i]).start()
+
+    def group(self, which, at, size, rows):
+        rights, highs, lows = [], [[] for _ in rows], [[] for _ in rows]
+        for i in range(size):
+            chunk = self.listed[which * self.pot.shape[0] * 2 + at + i]
+            self.copy(chunk).wait()
+            pots = self.pot[chunk // 2]
+            pot = jnp.where(lax.rem(chunk, 2) == 0, pots[:PERTS], pots[PERTS:])
+            rights.append(self.buf[chunk])
+            for no, (row, _) in enumerate(rows):
+                high, low = split_weights(pot, self.pick(chunk, row).astype(jnp.float32))
+                highs[no].append(high)
+                lows[no].append(low)
+        right = jnp.concatenate(rights + rights, axis=0)
+        for no, (_, spot) in enumerate(rows):
+            left = jnp.concatenate(highs[no] + lows[no], axis=1)
+            total = spot[...].reshape(left.shape[0], COLS) + jnp.dot(left, right, preferred_element_type=jnp.float32)
+            spot[...] = total.reshape(spot.shape)
+
+    def add(self, which, rows):
+        count = self.counted[which]
+        size = LARGEST
+        done = 0
+        while size:
+            times = (count - done) // size
+
+            @pl.loop(0, times)
+            def _(i, size=size, done=done):
+                self.group(which, done + i * size, size, rows)
+
+            done = done + times * size
+            size //= 2
+
+
+def fock_kernel(batches, share, facts_ref, pot_ref, picks_ref, phi_ref, out_ref,
+                total, pot_v, picks_v, listed, counted, buf, sems, in_sem, out_sem):
+    grid_pos = lax.axis_index("grid")
+    pot_copy = pltpu.make_async_copy(pot_ref, pot_v, in_sem.at[0])
+    pot_copy.start()
+    picks_copy = pltpu.make_async_copy(picks_ref, picks_v, in_sem.at[1])
+    picks_copy.start()
+    chunks = Chunks(batches, facts_ref, pot_v, lambda chunk, row: picks_v[chunk, row], phi_ref, listed, counted, buf, sems)
     base = 2 * grid_pos - REACH
-
-    def note(no, count):
-        lead = meta_ref[no // batches, lax.rem(no, batches), 0] - base
-        near = jnp.logical_and(lead >= 0, lead <= REACH + 1)
-
-        @pl.when(near)
-        def _():
-            chosen[count] = no
-
-        return count + near.astype(jnp.int32)
-
-    count = lax.fori_loop(0, SLOTS * batches, note, 0)
-
-    def fetch(i):
-        no = chosen[i]
-        return pltpu.make_async_copy(
-            phi_ref.at[no // batches, lax.rem(no, batches)], buf.at[lax.rem(i, DEPTH)], sems.at[lax.rem(i, DEPTH)])
-
-    for i in range(DEPTH - 1):
-        @pl.when(i < count)
-        def _():
-            fetch(i).start()
-
-    out_ref[...] = jnp.zeros_like(out_ref)
-    pick = one_hot(share, BLOCK, plane * share)
-
-    @pl.loop(0, count)
-    def _(i):
-        fetch(i).wait()
-
-        @pl.when(i + DEPTH - 1 < count)
-        def _():
-            fetch(i + DEPTH - 1).start()
-
-        no = chosen[i]
-        lead = meta_ref[no // batches, lax.rem(no, batches), 0] - base
-        few = meta_ref[no // batches, batches + lax.rem(no, batches), 0] <= POINTS // 2
-        here = buf.at[lax.rem(i, DEPTH)]
-        pot = joined(pot_ref[no])
-
-        def weights(offset):
-            own = here[:, pl.ds(pl.multiple_of(offset * BLOCK, BLOCK), BLOCK)]
-            picked = lax.dot_general(pick, own, NT, preferred_element_type=jnp.float32)
-            return split_weights(pot, picked, share)
-
-        def add(r, offset, value):
-            spot = out_ref.at[r, :, :, pl.ds(pl.multiple_of((REACH - offset) * BLOCK, BLOCK), COLS)]
-            spot[...] = spot[...] + value.reshape(PERTS, share, COLS)
+    leads = REACH + 2
+
+    for lead in range(leads):
+        counted[lead] = 0
+
+    @pl.loop(0, SLOTS * batches)
+    def _(no):
+        lead = chunks.start(no) - base
+        chunks.note(lead, no, jnp.logical_and(lead >= 0, lead < leads))
+
+    chunks.fetch(0)
+    chunks.fetch(1)
+    total[...] = jnp.zeros_like(total)
+    pot_copy.wait()
+    picks_copy.wait()
+
+    def spot(r, offset):
+        return total.at[r, :, :, pl.ds(pl.multiple_of((REACH - offset) * BLOCK, BLOCK), COLS)]
+
+    def out_copy(r, t):
+        cols = pl.ds(pl.multiple_of(t * BLOCK, BLOCK), BLOCK)
+        return pltpu.make_async_copy(total.at[r, :, :, cols], out_ref.at[r, :, :, cols], out_sem.at[r, t])
+
+    def leave(r, t):
+        @pl.when(facts_ref[SLOTS + r, t] == 0)
+        def _():
+            cols = pl.ds(pl.multiple_of(t * BLOCK, BLOCK), BLOCK)
+            total[r, :, :, cols] = jnp.zeros((PERTS, share, BLOCK), jnp.float32)
+
+        out_copy(r, t).start()
+
+    @pl.loop(0, leads)
+    def _(lead):
+        @pl.when(lead + 2 < leads)
+        def _():
+            chunks.fetch(lead + 2)
 
         both = jnp.logical_and(lead >= 1, lead <= REACH)
 
         @pl.when(both)
         def _():
             offset = REACH - lead
-            parts = [weights(offset), weights(offset + 1)]
-            rows = PERTS * share
-
-            def store(value):
-                add(0, offset, value[:rows])
-                add(1, offset + 1, value[rows:])
-
-            add_product(parts, here, few, store)
+            chunks.add(lead, [(0, spot(0, offset)), (1, spot(1, offset + 1))])
 
         @pl.when(jnp.logical_not(both))
         def _():
             r = jnp.where(lead == 0, 0, 1)
             offset = jnp.where(lead == 0, REACH, 0)
-            add_product([weights(offset)], here, few, lambda value: add(r, offset, value))
-
-    for r in range(2):
-        for t in range(BAND):
-            @pl.when(mask_ref[2 * grid_pos + r, t] == 0)
-            def _():
-                out_ref[r, :, :, t * BLOCK:(t + 1) * BLOCK] = jnp.zeros((PERTS, share, BLOCK), jnp.float32)
-
-
-def fock_own(meta_all, pair_mask, pot, phi_all, share):
+            chunks.add(lead, [(r, spot(r, offset))])
+
+        @pl.loop(lead, jnp.where(lead == REACH, BAND, jnp.minimum(lead + 1, REACH + 1)))
+        def _(t):
+            leave(0, t)
+
+        @pl.loop(jnp.maximum(lead - 1, 0), jnp.where(lead == REACH + 1, BAND, lead))
+        def _(t):
+            leave(1, t)
+
+    @pl.loop(0, BAND)
+    def _(t):
+        for r in range(2):
+            out_copy(r, t).wait()
+
+
+def chunk_scratch(slots, batches, cols, lists, dtype):
+    most = 2 * slots * batches
+    return [
+        pltpu.SMEM((lists * most,), jnp.int32),
+        pltpu.SMEM((lists,), jnp.int32),
+        pltpu.VMEM((most, CUT, cols), dtype),
+        pltpu.SemaphoreType.DMA((most,)),
+    ]
+
+
+def fock_own(facts, pot, picks, phi_all, share):
+    slots, batches, points, cols = phi_all.shape
+    far = pl.BlockSpec(memory_space=pl.ANY)
+    whole = (2, PERTS, share, WIDE)
+    dma = pltpu.SemaphoreType.DMA
+    return pl.pallas_call(
+        functools.partial(fock_kernel, batches, share),
+        out_shape=jax.ShapeDtypeStruct(whole, jnp.float32),
+        in_specs=[pl.BlockSpec(memory_space=pltpu.SMEM), far, far, far],
+        out_specs=far,
+        scratch_shapes=[
+            pltpu.VMEM(whole, jnp.float32), pltpu.VMEM(pot.shape, pot.dtype), pltpu.VMEM(picks.shape, picks.dtype),
+        ]
+        + chunk_scratch(slots, batches, cols, REACH + 2, phi_all.dtype)
+        + [dma((2,)), dma((2, BAND))],
+        compiler_params=pltpu.CompilerParams(vmem_limit_bytes=56 << 20),
+        cost_estimate=pl.CostEstimate(flops=20 * 10**9, bytes_accessed=20 * 10**6, transcendentals=0),
+        name="fock_own",
+    )(facts, pot, picks, phi_all)
+
+
+def far_kernel(batches, facts_ref, pot_ref, picks_ref, phi_ref, out_ref, listed, counted, buf, sems):
+    grid_pos = lax.axis_index("grid")
+    core = lax.rem(grid_pos, 2)
+    slot = jnp.where(core == 0, 4, 1)
+    far_start = 4 * (grid_pos // 2) - 1
+    chunks = Chunks(batches, facts_ref, pot_ref, lambda chunk, row: picks_ref[chunk - 2 * batches * slot], phi_ref,
+                    listed, counted, buf, sems)
+    counted[0] = 0
+
+    @pl.loop(0, batches)
+    def _(no):
+        chunks.note(0, slot * batches + no, chunks.start(slot * batches + no) == far_start)
+
+    chunks.fetch(0)
+    out_ref[...] = jnp.zeros_like(out_ref)
+    chunks.add(0, [(0, out_ref)])
+
+
+def fock_far(facts, pot, far_picks, phi_all, share):
     slots, batches, points, cols = phi_all.shape
     smem = pl.BlockSpec(memory_space=pltpu.SMEM)
     vmem = pl.BlockSpec(memory_space=pltpu.VMEM)
     return pl.pallas_call(
-        functools.partial(fock_kernel, batches, share),
-        out_shape=jax.ShapeDtypeStruct((2, PERTS, share, WIDE), jnp.float32),
-        in_specs=[smem, smem, vmem, pl.BlockSpec(memory_space=pl.ANY)],
+        functools.partial(far_kernel, batches),
+        out_shape=jax.ShapeDtypeStruct((PERTS, share, COLS), jnp.float32),
+        in_specs=[smem, vmem, vmem, pl.BlockSpec(memory_space=pl.ANY)],
         out_specs=vmem,
-        scratch_shapes=[
-            pltpu.SMEM((slots * batches,), jnp.int32),
-            pltpu.VMEM((DEPTH, points, cols), phi_all.dtype),
-            pltpu.SemaphoreType.DMA((DEPTH,)),
-        ],
-        compiler_params=pltpu.CompilerParams(vmem_limit_bytes=56 << 20),
-        cost_estimate=pl.CostEstimate(flops=20 * 10**9, bytes_accessed=20 * 10**6, transcendentals=0),
-        name="fock_own",
-    )(meta_all, pair_mask, pot, phi_all)
-
-
-def far_kernel(batches, share, meta_ref, pot_ref, phi_ref, out_ref, buf, sem):
-    grid_pos, plane = lax.axis_index("grid"), lax.axis_index("basis")
-    core = lax.rem(grid_pos, 2)
-    slot = jnp.where(core == 0, 4, 1)
-    far_start = 4 * (grid_pos // 2) - 1
-    out_ref[...] = jnp.zeros_like(out_ref)
-    pick = one_hot(share, BLOCK, plane * share)
-
-    @pl.loop(0, batches)
-    def _(no):
-        @pl.when(meta_ref[slot, no, 0] == far_start)
-        def _():
-            copy = pltpu.make_async_copy(phi_ref.at[slot, no], buf, sem)
-            copy.start()
-            copy.wait()
-            own = buf[:, pl.ds(pl.multiple_of(core * REACH * BLOCK, BLOCK), BLOCK)]
-            picked = lax.dot_general(pick, own, NT, preferred_element_type=jnp.float32)
-            parts = [split_weights(joined(pot_ref[slot * batches + no]), picked, share)]
-
-            def store(value):
-                out_ref[...] += value.reshape(PERTS, share, COLS)
-
-            add_product(parts, buf, meta_ref[slot, batches + no, 0] <= POINTS // 2, store)
-
-
-def fock_far(meta_all, pot, phi_all, share):
-    slots, batches, points, cols = phi_all.shape
-    smem = pl.BlockSpec(memory_space=pltpu.SMEM)
-    vmem = pl.BlockSpec(memory_space=pltpu.VMEM)
-    return pl.pallas_call(
-        functools.partial(far_kernel, batches, share),
-        out_shape=jax.ShapeDtypeStruct((PERTS, share, COLS), jnp.float32),
-        in_specs=[smem, vmem, pl.BlockSpec(memory_space=pl.ANY)],
-        out_specs=vmem,
-        scratch_shapes=[pltpu.VMEM((points, cols), phi_all.dtype), pltpu.SemaphoreType.DMA],
+        scratch_shapes=chunk_scratch(slots, batches, cols, 1, phi_all.dtype),
         compiler_params=pltpu.CompilerParams(vmem_limit_bytes=56 << 20),
         cost_estimate=pl.CostEstimate(flops=10**9, bytes_accessed=2 * 10**6, transcendentals=0),
         name="fock_far",
-    )(meta_all, pot, phi_all)
+    )(facts, pot, far_picks, phi_all)
 
 
 def shards(density, basis_vals, kernel, starts, counts, pair_mask):
@@ -579,13 +657,15 @@
     batches, share = basis_vals.shape[0], density.shape[2]
     grid_pos = lax.axis_index("grid")
     core = lax.rem(grid_pos, 2)
-    phi_all, meta_all, pot = potentials(
+    phi_all, facts, pot, picks, far_picks = potentials(
         basis_vals, density, starts, counts, pair_mask, kernel, grid_size // 2, planes)
     pot = pot.reshape(SLOTS * batches, 2 * PERTS, POINTS // 2)
-    far = fock_far(meta_all, pot, phi_all, share)
+    picks = picks.reshape(2 * SLOTS * batches, 2, share, POINTS // 2)
+    far_picks = far_picks.reshape(2 * batches, share, POINTS // 2)
+    far = fock_far(facts, pot, far_picks, phi_all, share)
     route = [(i, (i + 1) % grid_size if i % 2 else (i - 1) % grid_size) for i in range(grid_size)]
     arrived = lax.ppermute(far, "grid", route)
-    own = fock_own(meta_all, pair_mask, pot, phi_all, share)
+    own = fock_own(facts, pot, picks, phi_all, share)
     mask_row = lax.dynamic_slice(pair_mask, (2 * grid_pos + core, core * REACH), (1, WINDOW))[0]
     keep = jnp.repeat(mask_row, BLOCK).astype(jnp.float32)
     place = (core, 0, 0, core * REACH * BLOCK)

time: 128 us -> 120 us (0.938)
  the two profiles are of different devices: /device:TPU:9 before, /device:TPU:8 now
where the time goes in v3:
time: 120 us; the launch traced here: 119 us
  Pallas kernels  115 us (96%)
  other arithmetic  2.62 us (2%)
  local copies, waits for them, and re-layouts  1.48 us (1%)
    pallas_call x1, Pallas kernels, potentials(): pl.pallas_call(functools.partial(density_kernel, chips, planes, batches,...  78.9 us
    pallas_call x1, Pallas kernels, fock_own(): pl.pallas_call(functools.partial(fock_kernel, batches, share), out_shape=...  30.4 us
    pallas_call x1, Pallas kernels, fock_far(): pl.pallas_call(functools.partial(far_kernel, batches), out_shape=jax.Shap...  5.72 us
    dynamic_update_slice x1, other arithmetic, shards(): lax.dynamic_update_slice(own, present + (arrived * keep)[None], place)  2.43 us
  transfers between devices with their start and end apart: 1, of which 0 were waited for; matrix products, arithmetic and copies ran while one was open for 0% of the time, Pallas kernels for 25%

profile of v3, /device:TPU:8, one launch (start us, length us, event | category | flops | bytes accessed | tf_op | source)
XLA Modules:
  0.0 119.3 jit_solution(9026967697409798725)
XLA Ops:
  0.0 1.4 %copy.7.mask_ref = s32[64,11]{1,0:T(8,128)} copy(s32[64,11]{0,1:T(8,128)} %param.11) | data formatting | bytes 5632 | tf_op args[5]
  1.4 78.9 %potentials.1 = (bf16[6,8,256,768]{3,2,1,0:T(8,128)(2,1)}, s32[8,128]{1,0:T(8,128)}, f32[6,4,2,24,128]{4,3,2,1,0:T(8,128)}, bf16[6,8,2,2,32,128]{5,4,3,2,1,0:T(8,128)(2,1)}, bf16[8,2,32,128]{3,2,1,0:T(8,128)(2,1)}) custom-call(bf16[8,256,768]{2,1,0:T(8,128)(2,1)} %phi_ref.1, bf16[2,12,32,1408]{3,2,1,0:T(8,128)(2,1)} %dens_ref.1, s32[8]{0:T(128)} %starts_ref.1, ...), custom_call_target="tpu_custom_call" | custom-call | flops 16999999488 | bytes 50000000 | tf_op jit(solution)/shard_map/potentials/pallas_call | solution.py:401
  80.3 0.0 copy-start
  80.3 5.7 %fock_far.1 = f32[12,32,768]{2,1,0:T(8,128)} custom-call(s32[8,128]{1,0:T(8,128)} %get-tuple-element.10.facts_ref, f32[48,24,128]{2,1,0:T(8,128)} %bitcast.9, bf16[16,32,128]{2,1,0:T(8,128)(2,1)} %bitcast.11, bf16[6,8,256,768]{3,2,1,0:T(8,128)(2,1)} %get-tuple-element.13.phi_ref), custom_call_target="tpu_custom_call" | custom-call | flops 1000000000 | bytes 2000000 | tf_op jit(solution)/shard_map/fock_far/pallas_call | solution.py:643
  86.1 0.1 collective-permute-start
  86.2 0.0 copy-done
  86.2 0.2 convert_reduce_fusion
  86.4 0.1 broadcast_bitcast_fusion
  86.4 30.4 %fock_own.1 = f32[2,12,32,1408]{3,2,1,0:T(8,128)} custom-call(s32[8,128]{1,0:T(8,128)} %get-tuple-element.10.facts_ref, f32[48,24,128]{2,1,0:T(8,128)} %bitcast.10, bf16[96,2,32,128]{3,2,1,0:T(8,128)(2,1)} %bitcast.12, bf16[6,8,256,768]{3,2,1,0:T(8,128)(2,1)} %get-tuple-element.13.phi_ref), custom_call_target="tpu_custom_call" | custom-call | flops 20000000000 | bytes 20000000 | tf_op jit(solution)/shard_map/fock_own/pallas_call | solution.py:605
  116.8 0.0 collective-permute-done
  116.8 2.4 %fusion = f32[2,12,32,1408]{3,2,1,0:T(8,128)} fusion(f32[2,12,32,1408]{3,2,1,0:T(8,128)} %fock_own.1, s32[]{:T(128)S(6)} %select_n.14, s32[]{:T(128)S(6)} %select_n.15, f32[12,32,768]{2,1,0:T(8,128)S(1)} %collective-permute-done, f32[768]{0:T(1024)S(1)} %broadcast_bitcast_fusion), kind=kLoop, calls=%fused_computation.1 | loop fusion | flops 589824 | bytes 3542024 | tf_op jit(solution)/shard_map/dynamic_update_slice | solution.py:673
Async XLA Ops:
  80.3 5.9 %copy-start = (s32[64,11]{0,1:T(8,128)S(1)}, s32[64,11]{0,1:T(8,128)}, u32[]{:S(2)}) copy-start(s32[64,11]{0,1:T(8,128)} %param.11) | copy-start | bytes 8452
  86.1 30.8 %collective-permute-start = (f32[12,32,768]{2,1,0:T(8,128)}, f32[12,32,768]{2,1,0:T(8,128)S(1)}, u32[]{:S(2)}, u32[]{:S(2)}) collective-permute-start(f32[12,32,768]{2,1,0:T(8,128)} %fock_far.1), channel_id=1, source_target_pairs={{0,124},{4,8},{8,4},{12,16},{16,12},{20,24},{24,20},{28,32},{32,28... | collective-permute-start | bytes 3538952 | tf_op jit(solution)/shard_map/ppermute | solution.py:667

commit v4 on v3

--- a/solution.py
+++ b/solution.py
@@ -154,7 +154,7 @@
         row = 2 * grid_pos + r
         for t in range(BAND):
             block = left_v[r, :, :, t * BLOCK:(t + 1) * BLOCK].reshape(rows_all, BLOCK)
-            dens_v[r, t, :rows_all, :] = masked(block, mask_s[row, t])
+            dens_v[r, t, :rows_all, :] = masked(block, mask_s[t, row])
             dens_v[r, t, rows_all:, :] = one_hot(share, BLOCK, (REACH - t) * BLOCK + plane * share)
     far_v[rows_all:, :] = one_hot(share, COLS, core * REACH * BLOCK + plane * share)
 
@@ -166,7 +166,7 @@
         facts = jnp.where(line == slot, meta_all_v[slot], facts)
     for r in range(2):
         for t in range(BAND):
-            facts = jnp.where(jnp.logical_and(line == SLOTS + r, lane == t), mask_s[2 * grid_pos + r, t], facts)
+            facts = jnp.where(jnp.logical_and(line == SLOTS + r, lane == t), mask_s[t, 2 * grid_pos + r], facts)
     facts_v[...] = facts
     to_smem = pltpu.make_async_copy(facts_v, meta_s, own_sem.at[3])
     to_smem.start()
@@ -181,33 +181,38 @@
         sums = jnp.sum(mixed[:rows_all].reshape(PERTS, share, POINTS) * picked[None], axis=1)
         return jnp.concatenate([sums[:, :cut], sums[:, cut:]], axis=0)
 
-    def rho_part(slot, no):
-        start = meta_s[slot, no]
-        lhs, keeps = [], []
-        for r in range(2):
-            offset = 2 * grid_pos + r - start
-            inside = jnp.clip(offset, 0, WINDOW - 1)
-            keeps.append(same(offset, inside))
-            lhs.append(jnp.concatenate([dens_v[r, REACH - inside + c] for c in range(WINDOW)], axis=1))
+    def spread_rows(slot, no, r):
+        offset = 2 * grid_pos + r - meta_s[slot, no]
+        inside = jnp.clip(offset, 0, WINDOW - 1)
+        lhs = jnp.concatenate([dens_v[r, REACH - inside + c] for c in range(WINDOW)], axis=1)
+        return lhs, same(offset, inside)
+
+    def rho_part(slot, no, blocks):
+        out_copy(slot, no).start()
+        lhs, keeps = zip(*[spread_rows(slot, no, r) for r in blocks])
         mixed = lax.dot_general(jnp.concatenate(lhs, axis=0), phi_v[slot, no], NT, preferred_element_type=jnp.float32)
         total = None
-        for r in range(2):
+        for i, r in enumerate(blocks):
             def keep_picks(h, value, r=r):
                 picks_v[slot, no, h, r] = value
 
-            term = reduced(mixed[r * (rows_all + share):(r + 1) * (rows_all + share)], keep_picks) * keeps[r]
+            term = reduced(mixed[i * (rows_all + share):(i + 1) * (rows_all + share)], keep_picks) * keeps[i]
             total = term if total is None else total + term
         part[slot, no] = total
 
     far_start = 4 * chip - 1
 
-    def rho_far(slot, no):
-        mixed = lax.dot_general(far_v[...], phi_v[slot, no], NT, preferred_element_type=jnp.float32)
-
-        def keep_picks(h, value):
-            far_picks_v[no, h] = value
-
-        part[slot, no] = part[slot, no] + reduced(mixed, keep_picks) * same(meta_s[slot, no], far_start)
+    def rho_far(pair):
+        phi = phi_v[far_slot, pl.ds(2 * pair, 2)].reshape(2 * POINTS, COLS)
+        mixed = lax.dot_general(far_v[...], phi, NT, preferred_element_type=jnp.float32)
+        for i in range(2):
+            no = 2 * pair + i
+
+            def keep_picks(h, value, no=no):
+                far_picks_v[no, h] = value
+
+            term = reduced(mixed[:, i * POINTS:(i + 1) * POINTS], keep_picks)
+            part[far_slot, no] = part[far_slot, no] + term * same(meta_s[far_slot, no], far_start)
 
     def part_copy(slot, no):
         back = 2 * (2 - slot // 2) + core
@@ -227,99 +232,109 @@
         def _():
             gathered[own_slot, plane, lax.rem(no, per_plane)] = part[slot, no]
 
-    def items(n, act):
-        @pl.loop(0, 8)
+    def pair(n, crossed, late):
+        lead = jnp.where(crossed, core, 0)
+        at = jnp.where(late, there, first)
+        return tuple((4 * way + jnp.where(crossed, 1 - core, core), at + piece(way, n)) for way in (lead, 1 - lead))
+
+    def items_before(m, act):
+        odd = lax.rem(m, 2) == 1
+
+        @pl.loop(0, 3)
         def _(item):
-            kind, way = item // 2, lax.rem(item, 2)
-            late = jnp.where(kind == 0, 0, jnp.where(kind == 3, 2, 1))
-            came = n - late
-            slot = 4 * way + jnp.where(kind <= 1, core, 1 - core)
-            at = jnp.where(lax.rem(kind, 2) == 0, first, there) + piece(way, jnp.maximum(came, 0))
-
-            @pl.when(jnp.logical_and(came >= 0, came < half))
+            mine = 2 * (m + 1) + item - 1
+            slot = jnp.where(mine < half, own_slot, 5 - own_slot)
+            at = 2 * lax.rem(mine, half)
+            arrived = pair(jnp.maximum(m - 1, 0) // 2, False, False)
+            is_own = item > 0
+            chosen = tuple((jnp.where(is_own, slot, s), jnp.where(is_own, at + i, no)) for i, (s, no) in enumerate(arrived))
+
+            @pl.when(jnp.logical_or(jnp.logical_and(is_own, m <= 2),
+                                    jnp.logical_and(jnp.logical_not(is_own), jnp.logical_and(odd, m <= 2 * half - 1))))
             def _():
-                act(slot, at)
-
-    def send_near(slot, no):
-        @pl.when(slot != far_slot)
-        def _():
-            send_part(slot, no)
-
-    @pl.loop(0, batches)
-    def _(no):
-        out_copy(own_slot, no).start()
-        rho_part(own_slot, no)
-
-    @pl.loop(0, half + 2)
-    def _(n):
-        @pl.when(n < half)
-        def _():
-            for h in range(2):
-                for way in range(2):
-                    y_copy(way, n, h).wait_recv()
-                    z_copy(way, n, h).start()
-                    c_copy(way, n, h).start()
+                act(chosen, False)
+
+        @pl.when(m >= 2)
+        def _():
+            act(pair((m - 2 - lax.rem(m, 2)) // 2, True, odd), True)
+
+    def items_after(m, act):
+        @pl.when(jnp.logical_and(m >= 2, jnp.logical_and(lax.rem(m, 2) == 0, m <= 2 * half)))
+        def _():
+            act(pair((m - 2) // 2, False, True), False)
+
+    def compute(batch_pair, crossed):
+        rho_part(*batch_pair[0], (0, 1))
+        rho_part(*batch_pair[1], (1 - core,) if crossed else (0, 1))
+
+    def send(batch_pair, crossed):
+        for slot, no in batch_pair:
+            @pl.when(slot != far_slot)
+            def _():
+                send_part(slot, no)
+
+    @pl.loop(0, 2 * half + 3)
+    def _(step):
+        m = step - 1
+
+        @pl.when(jnp.logical_and(m >= 0, m < 2 * half))
+        def _():
+            n, h = m // 2, lax.rem(m, 2)
             for way in range(2):
-                out_copy(4 * way + core, first + piece(way, n)).start()
-
-        @pl.when(jnp.logical_and(n >= 1, n <= half))
-        def _():
-            for h in range(2):
-                for way in range(2):
-                    z_copy(way, n - 1, h).wait_recv()
-                    c_copy(way, half + n - 1, h).start()
-            for way in range(2):
-                out_copy(4 * way + core, there + piece(way, n - 1)).start()
+                y_copy(way, n, h).wait_recv()
+                z_copy(way, n, h).start()
+                c_copy(way, n, h).start()
+
+        @pl.when(jnp.logical_or(m == 1, m == 2))
+        def _():
+            for i in range(half):
+                core_copy((m - 1) * half + i).wait_recv()
+
+        @pl.when(m >= 2)
+        def _():
+            late = lax.rem(m, 2)
             for way in range(2):
                 for h in range(2):
-                    c_copy(way, n - 1, h).wait_recv()
-                out_copy(4 * way + 1 - core, first + piece(way, n - 1)).start()
-
-        @pl.when(n >= 2)
-        def _():
+                    c_copy(way, late * half + (m - 2 - late) // 2, h).wait_recv()
+
+        @pl.when(m == half + 1)
+        def _():
+            @pl.loop(0, half + 2)
+            def _(before):
+                items_before(before - 1, send)
+                items_after(before - 1, send)
+
+        items_before(m, compute)
+
+        @pl.when(m > half)
+        def _():
+            items_before(m, send)
+
+        @pl.when(jnp.logical_and(m >= 1, m <= 2 * half))
+        def _():
+            n, h = (m - 1) // 2, lax.rem(m - 1, 2)
             for way in range(2):
-                for h in range(2):
-                    c_copy(way, half + n - 2, h).wait_recv()
-                out_copy(4 * way + 1 - core, there + piece(way, n - 2)).start()
-
-        @pl.when(n == half)
-        def _():
-            @pl.loop(0, batches)
-            def _(no):
-                for slot in range(2):
-                    send_part(2 + slot, no)
-
-            @pl.loop(0, half)
-            def _(m):
-                items(m, send_near)
-
-        items(n, rho_part)
-
-        @pl.when(n >= half)
-        def _():
-            items(n, send_near)
-
-        @pl.when(n == 0)
-        def _():
-            @pl.loop(0, batches)
-            def _(no):
-                core_copy(no).wait_recv()
-                out_copy(5 - own_slot, no).start()
-                rho_part(5 - own_slot, no)
-
-        @pl.when(n == half)
-        def _():
-            far_copy.wait_recv()
-            far_row = jnp.where(core == 0, jnp.maximum(2 * grid_pos - 1, 0), jnp.minimum(2 * grid_pos + 2, 4 * chips - 1))
-            for t in range(WINDOW):
-                block = left_far[:, :, t * BLOCK:(t + 1) * BLOCK].reshape(rows_all, BLOCK)
-                keep = mask_s[far_row, jnp.where(core == 0, REACH, 0) + t]
-                far_v[:rows_all, t * BLOCK:(t + 1) * BLOCK] = masked(block, keep)
-
-            @pl.loop(0, batches)
-            def _(no):
-                rho_far(far_slot, no)
-                send_part(far_slot, no)
+                z_copy(way, n, h).wait_recv()
+                c_copy(way, half + n, h).start()
+
+        items_after(m, compute)
+
+        @pl.when(m > half)
+        def _():
+            items_after(m, send)
+
+    far_copy.wait_recv()
+    far_row = jnp.where(core == 0, jnp.maximum(2 * grid_pos - 1, 0), jnp.minimum(2 * grid_pos + 2, 4 * chips - 1))
+    for t in range(WINDOW):
+        block = left_far[:, :, t * BLOCK:(t + 1) * BLOCK].reshape(rows_all, BLOCK)
+        keep = mask_s[jnp.where(core == 0, REACH, 0) + t, far_row]
+        far_v[:rows_all, t * BLOCK:(t + 1) * BLOCK] = masked(block, keep)
+
+    @pl.loop(0, half)
+    def _(two):
+        rho_far(two)
+        for i in range(2):
+            send_part(far_slot, 2 * two + i)
 
     picks_out = pltpu.make_async_copy(picks_v, picks_ref, own_sem.at[1])
     picks_out.start()
@@ -494,10 +509,12 @@
                 highs[no].append(high)
                 lows[no].append(low)
         right = jnp.concatenate(rights + rights, axis=0)
+        left = jnp.concatenate(
+            [jnp.concatenate(high + low, axis=1) for high, low in zip(highs, lows)], axis=0)
+        total = jnp.dot(left, right, preferred_element_type=jnp.float32)
+        depth = left.shape[0] // len(rows)
         for no, (_, spot) in enumerate(rows):
-            left = jnp.concatenate(highs[no] + lows[no], axis=1)
-            total = spot[...].reshape(left.shape[0], COLS) + jnp.dot(left, right, preferred_element_type=jnp.float32)
-            spot[...] = total.reshape(spot.shape)
+            spot[...] = spot[...] + total[no * depth:(no + 1) * depth].reshape(spot.shape)
 
     def add(self, which, rows):
         count = self.counted[which]
@@ -658,7 +675,7 @@
     grid_pos = lax.axis_index("grid")
     core = lax.rem(grid_pos, 2)
     phi_all, facts, pot, picks, far_picks = potentials(
-        basis_vals, density, starts, counts, pair_mask, kernel, grid_size // 2, planes)
+        basis_vals, density, starts, counts, pair_mask.T, kernel, grid_size // 2, planes)
     pot = pot.reshape(SLOTS * batches, 2 * PERTS, POINTS // 2)
     picks = picks.reshape(2 * SLOTS * batches, 2, share, POINTS // 2)
     far_picks = far_picks.reshape(2 * batches, share, POINTS // 2)

time: 120 us -> 115 us (0.958)
  the two profiles are of different devices: /device:TPU:8 before, /device:TPU:9 now
where the time goes in v4:
time: 115 us; the launch traced here: 113 us
  Pallas kernels  110 us (96%)
  other arithmetic  2.62 us (2%)
    pallas_call x1, Pallas kernels, potentials(): pl.pallas_call(functools.partial(density_kernel, chips, planes, batches,...  76.9 us
    pallas_call x1, Pallas kernels, fock_own(): pl.pallas_call(functools.partial(fock_kernel, batches, share), out_shape=...  28 us
    pallas_call x1, Pallas kernels, fock_far(): pl.pallas_call(functools.partial(far_kernel, batches), out_shape=jax.Shap...  5 us
    dynamic_update_slice x1, other arithmetic, shards(): lax.dynamic_update_slice(own, present + (arrived * keep)[None], place)  2.43 us
  transfers between devices with their start and end apart: 1, of which 0 were waited for; matrix products, arithmetic and copies ran while one was open for 0% of the time, Pallas kernels for 25%

profile of v4, /device:TPU:9, one launch (start us, length us, event | category | flops | bytes accessed | tf_op | source)
XLA Modules:
  0.0 112.8 jit_solution(128133130914052362)
XLA Ops:
  0.0 76.9 %potentials.1 = (bf16[6,8,256,768]{3,2,1,0:T(8,128)(2,1)}, s32[8,128]{1,0:T(8,128)}, f32[6,4,2,24,128]{4,3,2,1,0:T(8,128)}, bf16[6,8,2,2,32,128]{5,4,3,2,1,0:T(8,128)(2,1)}, bf16[8,2,32,128]{3,2,1,0:T(8,128)(2,1)}) custom-call(bf16[8,256,768]{2,1,0:T(8,128)(2,1)} %phi_ref.1, bf16[2,12,32,1408]{3,2,1,0:T(8,128)(2,1)} %dens_ref.1, s32[8]{0:T(128)} %starts_ref.1, ...), custom_call_target="tpu_custom_call" | custom-call | flops 16999999488 | bytes 50000000 | tf_op jit(solution)/shard_map/potentials/pallas_call | solution.py:416
  76.9 0.0 copy-start
  76.9 5.0 %fock_far.1 = f32[12,32,768]{2,1,0:T(8,128)} custom-call(s32[8,128]{1,0:T(8,128)} %get-tuple-element.10.facts_ref, f32[48,24,128]{2,1,0:T(8,128)} %bitcast.10, bf16[16,32,128]{2,1,0:T(8,128)(2,1)} %bitcast.12, bf16[6,8,256,768]{3,2,1,0:T(8,128)(2,1)} %get-tuple-element.13.phi_ref), custom_call_target="tpu_custom_call" | custom-call | flops 1000000000 | bytes 2000000 | tf_op jit(solution)/shard_map/fock_far/pallas_call | solution.py:660
  81.9 0.1 collective-permute-start
  82.0 0.0 copy-done
  82.0 0.2 convert_reduce_fusion
  82.2 0.1 broadcast_bitcast_fusion
  82.3 28.0 %fock_own.1 = f32[2,12,32,1408]{3,2,1,0:T(8,128)} custom-call(s32[8,128]{1,0:T(8,128)} %get-tuple-element.10.facts_ref, f32[48,24,128]{2,1,0:T(8,128)} %bitcast.11, bf16[96,2,32,128]{3,2,1,0:T(8,128)(2,1)} %bitcast.14, bf16[6,8,256,768]{3,2,1,0:T(8,128)(2,1)} %get-tuple-element.13.phi_ref), custom_call_target="tpu_custom_call" | custom-call | flops 20000000000 | bytes 20000000 | tf_op jit(solution)/shard_map/fock_own/pallas_call | solution.py:622
  110.3 0.0 collective-permute-done
  110.4 2.4 %fusion = f32[2,12,32,1408]{3,2,1,0:T(8,128)} fusion(f32[2,12,32,1408]{3,2,1,0:T(8,128)} %fock_own.1, s32[]{:T(128)S(6)} %select_n.14, s32[]{:T(128)S(6)} %select_n.15, f32[12,32,768]{2,1,0:T(8,128)S(1)} %collective-permute-done, f32[768]{0:T(1024)S(1)} %broadcast_bitcast_fusion), kind=kLoop, calls=%fused_computation.1 | loop fusion | flops 589824 | bytes 3542024 | tf_op jit(solution)/shard_map/dynamic_update_slice | solution.py:690
Async XLA Ops:
  76.9 5.1 %copy-start = (s32[64,11]{0,1:T(8,128)S(1)}, s32[64,11]{0,1:T(8,128)}, u32[]{:S(2)}) copy-start(s32[64,11]{0,1:T(8,128)} %param.11) | copy-start | bytes 8452
  81.9 28.4 %collective-permute-start = (f32[12,32,768]{2,1,0:T(8,128)}, f32[12,32,768]{2,1,0:T(8,128)S(1)}, u32[]{:S(2)}, u32[]{:S(2)}) collective-permute-start(f32[12,32,768]{2,1,0:T(8,128)} %fock_far.1), channel_id=1, source_target_pairs={{0,124},{4,8},{8,4},{12,16},{16,12},{20,24},{24,20},{28,32},{32,28... | collective-permute-start | bytes 3538952 | tf_op jit(solution)/shard_map/ppermute | solution.py:684

commit v5 on v4

--- a/solution.py
+++ b/solution.py
@@ -30,8 +30,8 @@
     chips, planes, batches, share,
     phi_ref, dens_ref, starts_ref, counts_ref, mask_ref, kern_ref,
     all_ref, facts_ref, pot_ref, picks_ref, far_picks_ref,
-    phi_v, dens_v, far_v, left_v, left_far, meta_v, meta_all_v, facts_v, meta_s, mask_s, picks_v, far_picks_v, part, gathered, pot_v,
-    own_sem, out_sem, core_s, core_r, y_s, y_r, z_s, z_r, c_s, c_r, m_s, m_r, f_sem, a_s, a_r, b_s, b_r,
+    phi_v, dens_v, far_v, left_v, left_far, meta_v, meta_all_v, facts_v, meta_s, mask_s, picks_v, far_picks_v, part, mate, gathered, pot_v,
+    own_sem, out_sem, core_s, core_r, y_s, y_r, z_s, z_r, c_s, c_r, m_s, m_r, f_sem, k_s, k_r, a_s, a_r, b_s, b_r, g_s, g_r,
 ):
     grid_pos, plane = lax.axis_index("grid"), lax.axis_index("basis")
     chip, core = grid_pos // 2, lax.rem(grid_pos, 2)
@@ -54,17 +54,18 @@
         return pltpu.make_async_remote_copy(
             src_ref=src, dst_ref=dst, send_sem=send, recv_sem=recv, device_id=to, device_id_type=MESH)
 
-    def is_other(slot, at_plane):
-        return jnp.logical_or(slot != own_slot, at_plane != plane)
-
-    def for_others(act):
-        @pl.loop(0, SLOTS * planes)
+    def is_other(d, at_plane):
+        return jnp.logical_or(d != 1, at_plane != plane)
+
+    def for_others(act, order=(0, 2, 1)):
+        @pl.loop(0, 3 * planes)
         def _(no):
-            slot, at_plane = no // planes, lax.rem(no, planes)
-
-            @pl.when(is_other(slot, at_plane))
+            turn, at_plane = no // planes, lax.rem(no, planes)
+            d = jnp.where(turn == 0, order[0], jnp.where(turn == 1, order[1], order[2]))
+
+            @pl.when(is_other(d, at_plane))
             def _():
-                act(slot, at_plane)
+                act(d, at_plane)
 
     own_copy = pltpu.make_async_copy(phi_ref, phi_v.at[own_slot], own_sem.at[0])
     own_copy.start()
@@ -214,23 +215,28 @@
             term = reduced(mixed[:, i * POINTS:(i + 1) * POINTS], keep_picks)
             part[far_slot, no] = part[far_slot, no] + term * same(meta_s[far_slot, no], far_start)
 
-    def part_copy(slot, no):
-        back = 2 * (2 - slot // 2) + core
+    def mate_copy(d, no):
+        return remote(part.at[2 * d + 1 - core, no], mate.at[d, no], k_s.at[d, no], k_r.at[d, no], other)
+
+    def part_copy(d, no):
         keeper = no // per_plane
         which = lax.rem(no, per_plane)
-        return remote(part.at[slot, no], gathered.at[back, plane, which], a_s.at[slot, no], a_r.at[back, plane, which],
-                      device(slot, keeper))
-
-    def send_part(slot, no):
-        away = is_other(slot, no // per_plane)
+        return remote(part.at[2 * d + core, no], gathered.at[2 - d, plane, which], a_s.at[d, no], a_r.at[2 - d, plane, which],
+                      device(2 * d + core, keeper))
+
+    def combine(d, no):
+        slot = 2 * d + core
+        pltpu.make_async_copy(part.at[slot, no], mate.at[d, no], k_r.at[d, no]).wait()
+        part[slot, no] = part[slot, no] + mate[d, no]
+        away = is_other(d, no // per_plane)
 
         @pl.when(away)
         def _():
-            part_copy(slot, no).start()
+            part_copy(d, no).start()
 
         @pl.when(jnp.logical_not(away))
         def _():
-            gathered[own_slot, plane, lax.rem(no, per_plane)] = part[slot, no]
+            gathered[1, plane, lax.rem(no, per_plane)] = part[slot, no]
 
     def pair(n, crossed, late):
         lead = jnp.where(crossed, core, 0)
@@ -266,12 +272,17 @@
     def compute(batch_pair, crossed):
         rho_part(*batch_pair[0], (0, 1))
         rho_part(*batch_pair[1], (1 - core,) if crossed else (0, 1))
-
-    def send(batch_pair, crossed):
         for slot, no in batch_pair:
+            @pl.when(lax.rem(slot, 2) != core)
+            def _():
+                mate_copy(slot // 2, no).start()
+
+    def combine_pair(m):
+        late = jnp.where(lax.rem(m, 2) == 0, 1, 0)
+        for slot, no in pair((m - 3 - late) // 2, False, late == 1):
             @pl.when(slot != far_slot)
             def _():
-                send_part(slot, no)
+                combine(slot // 2, no)
 
     @pl.loop(0, 2 * half + 3)
     def _(step):
@@ -299,16 +310,15 @@
 
         @pl.when(m == half + 1)
         def _():
-            @pl.loop(0, half + 2)
+            @pl.loop(0, batches)
+            def _(no):
+                combine(1, no)
+
+            @pl.loop(3, half + 1)
             def _(before):
-                items_before(before - 1, send)
-                items_after(before - 1, send)
+                combine_pair(before)
 
         items_before(m, compute)
-
-        @pl.when(m > half)
-        def _():
-            items_before(m, send)
 
         @pl.when(jnp.logical_and(m >= 1, m <= 2 * half))
         def _():
@@ -321,8 +331,9 @@
 
         @pl.when(m > half)
         def _():
-            items_after(m, send)
-
+            combine_pair(m)
+
+    combine_pair(2 * half + 2)
     far_copy.wait_recv()
     far_row = jnp.where(core == 0, jnp.maximum(2 * grid_pos - 1, 0), jnp.minimum(2 * grid_pos + 2, 4 * chips - 1))
     for t in range(WINDOW):
@@ -334,35 +345,41 @@
     def _(two):
         rho_far(two)
         for i in range(2):
-            send_part(far_slot, 2 * two + i)
+            combine(far_slot // 2, 2 * two + i)
 
     picks_out = pltpu.make_async_copy(picks_v, picks_ref, own_sem.at[1])
     picks_out.start()
     far_picks_out = pltpu.make_async_copy(far_picks_v, far_picks_ref, own_sem.at[2])
     far_picks_out.start()
 
-    def pot_copy(slot, at_plane):
-        back = 2 * (2 - slot // 2) + core
-        return remote(pot_v, pot_ref.at[back, plane], b_s.at[slot, at_plane], b_r.at[back, plane],
-                      device(slot, at_plane))
-
-    def wait_parts(slot, at_plane):
+    def pot_copy(d, at_plane):
+        return remote(pot_v, pot_ref.at[2 * (2 - d) + core, plane], b_s.at[d, at_plane], b_r.at[2 - d, plane],
+                      device(2 * d + core, at_plane))
+
+    def cross_copy(d, at_plane):
+        where = pot_ref.at[2 * d + core, at_plane]
+        return remote(where, where, g_s.at[d, at_plane], g_r.at[d, at_plane], other)
+
+    own_cross = remote(pot_v, pot_ref.at[own_slot, plane], g_s.at[1, plane], g_r.at[1, plane], other)
+
+    def wait_parts(d, at_plane):
         for which in range(per_plane):
-            pltpu.make_async_copy(part.at[0, 0], gathered.at[slot, at_plane, which], a_r.at[slot, at_plane, which]).wait()
+            pltpu.make_async_copy(part.at[0, 0], gathered.at[d, at_plane, which], a_r.at[d, at_plane, which]).wait()
 
     for_others(wait_parts)
     points = lax.broadcasted_iota(jnp.int32, (1, POINTS), 1)
     for no in range(per_plane):
         rho = gathered[0, 0, no]
-        for slot in range(SLOTS):
+        for d in range(3):
             for at_plane in range(planes):
-                if slot or at_plane:
-                    rho = rho + gathered[slot, at_plane, no]
+                if d or at_plane:
+                    rho = rho + gathered[d, at_plane, no]
         mine = per_plane * plane + no
         live = jnp.clip(counts_ref[mine] - points, 0, 1).astype(jnp.float32)
         factor = jnp.broadcast_to(kern_ref[pl.ds(mine, 1), :] * live, (PERTS, POINTS))
         pot_v[no] = rho * jnp.concatenate([factor[:, :cut], factor[:, cut:]], axis=0)
-    for_others(lambda slot, at_plane: pot_copy(slot, at_plane).start())
+    for_others(lambda d, at_plane: pot_copy(d, at_plane).start())
+    own_cross.start()
     pot_own = pltpu.make_async_copy(pot_v, pot_ref.at[own_slot, plane], own_sem.at[0])
     pot_own.start()
 
@@ -380,10 +397,12 @@
         core_copy(no).wait_send()
         for slot in range(SLOTS):
             out_copy(slot, no).wait()
-
-            @pl.when(is_other(slot, no // per_plane))
+        for d in range(3):
+            mate_copy(d, no).wait_send()
+
+            @pl.when(is_other(d, no // per_plane))
             def _():
-                part_copy(slot, no).wait_send()
+                part_copy(d, no).wait_send()
 
     @pl.loop(0, half)
     def _(n):
@@ -394,10 +413,20 @@
                 c_copy(way, n, h).wait_send()
                 c_copy(way, half + n, h).wait_send()
 
-    for_others(lambda slot, at_plane: pltpu.make_async_copy(
-        pot_v, pot_ref.at[slot, at_plane], b_r.at[slot, at_plane]).wait())
+    def pass_on(d, at_plane):
+        pltpu.make_async_copy(pot_v, pot_ref.at[2 * d + core, at_plane], b_r.at[d, at_plane]).wait()
+        cross_copy(d, at_plane).start()
+
+    for_others(pass_on, (1, 0, 2))
+
+    @pl.loop(0, 3 * planes)
+    def _(no):
+        cross_copy(no // planes, lax.rem(no, planes)).wait_recv()
+
     pot_own.wait()
-    for_others(lambda slot, at_plane: pot_copy(slot, at_plane).wait_send())
+    own_cross.wait_send()
+    for_others(lambda d, at_plane: cross_copy(d, at_plane).wait_send())
+    for_others(lambda d, at_plane: pot_copy(d, at_plane).wait_send())
 
 
 def potentials(phi, density, starts, counts, pair_mask, kern, chips, planes):
@@ -438,12 +467,14 @@
             pltpu.VMEM(picks, phi.dtype),
             pltpu.VMEM(far_picks, phi.dtype),
             pltpu.VMEM((SLOTS, batches) + row_pair, f32),
-            pltpu.VMEM((SLOTS, planes, per_plane) + row_pair, f32),
+            pltpu.VMEM((3, batches) + row_pair, f32),
+            pltpu.VMEM((3, planes, per_plane) + row_pair, f32),
             pltpu.VMEM((per_plane,) + row_pair, f32),
             dma((5,)), dma((SLOTS, batches)), dma((batches,)), dma((batches,)),
             dma((2, half, 2)), dma((2, half, 2)), dma((2, half, 2)), dma((2, half, 2)),
             dma((2, batches, 2)), dma((2, batches, 2)), dma((5,)), dma((5,)), dma((2,)),
-            dma((SLOTS, batches)), dma((SLOTS, planes, per_plane)), dma((SLOTS, planes)), dma((SLOTS, planes)),
+            dma((3, batches)), dma((3, batches)), dma((3, batches)), dma((3, planes, per_plane)),
+            dma((3, planes)), dma((3, planes)), dma((3, planes)), dma((3, planes)),
         ],
         compiler_params=pltpu.CompilerParams(collective_id=0, has_side_effects=True, vmem_limit_bytes=56 << 20),
         cost_estimate=pl.CostEstimate(flops=17 * 10**9, bytes_accessed=50 * 10**6, transcendentals=0),
@@ -463,7 +494,7 @@
 
 
 CUT = POINTS // 2
-LARGEST = 4
+LARGEST = 8
 
 
 class Chunks:
@@ -635,12 +666,17 @@
     )(facts, pot, picks, phi_all)
 
 
-def far_kernel(batches, facts_ref, pot_ref, picks_ref, phi_ref, out_ref, listed, counted, buf, sems):
+def far_kernel(batches, facts_ref, pot_ref, picks_ref, phi_ref, out_ref, pot_v, picks_v, listed, counted, buf, sems, in_sem):
     grid_pos = lax.axis_index("grid")
     core = lax.rem(grid_pos, 2)
     slot = jnp.where(core == 0, 4, 1)
     far_start = 4 * (grid_pos // 2) - 1
-    chunks = Chunks(batches, facts_ref, pot_ref, lambda chunk, row: picks_ref[chunk - 2 * batches * slot], phi_ref,
+    own = pl.ds(slot * batches, batches)
+    pot_copy = pltpu.make_async_copy(pot_ref.at[own], pot_v.at[own], in_sem.at[0])
+    pot_copy.start()
+    picks_copy = pltpu.make_async_copy(picks_ref, picks_v, in_sem.at[1])
+    picks_copy.start()
+    chunks = Chunks(batches, facts_ref, pot_v, lambda chunk, row: picks_v[chunk - 2 * batches * slot], phi_ref,
                     listed, counted, buf, sems)
     counted[0] = 0
 
@@ -650,19 +686,24 @@
 
     chunks.fetch(0)
     out_ref[...] = jnp.zeros_like(out_ref)
+    pot_copy.wait()
+    picks_copy.wait()
     chunks.add(0, [(0, out_ref)])
 
 
 def fock_far(facts, pot, far_picks, phi_all, share):
     slots, batches, points, cols = phi_all.shape
     smem = pl.BlockSpec(memory_space=pltpu.SMEM)
+    far = pl.BlockSpec(memory_space=pl.ANY)
     vmem = pl.BlockSpec(memory_space=pltpu.VMEM)
     return pl.pallas_call(
         functools.partial(far_kernel, batches),
         out_shape=jax.ShapeDtypeStruct((PERTS, share, COLS), jnp.float32),
-        in_specs=[smem, vmem, vmem, pl.BlockSpec(memory_space=pl.ANY)],
+        in_specs=[smem, far, far, far],
         out_specs=vmem,
-        scratch_shapes=chunk_scratch(slots, batches, cols, 1, phi_all.dtype),
+        scratch_shapes=[pltpu.VMEM(pot.shape, pot.dtype), pltpu.VMEM(far_picks.shape, far_picks.dtype)]
+        + chunk_scratch(slots, batches, cols, 1, phi_all.dtype)
+        + [pltpu.SemaphoreType.DMA((2,))],
         compiler_params=pltpu.CompilerParams(vmem_limit_bytes=56 << 20),
         cost_estimate=pl.CostEstimate(flops=10**9, bytes_accessed=2 * 10**6, transcendentals=0),
         name="fock_far",

time: 115 us -> 112 us (0.974)
  Pallas kernels: 110 us -> 107 us
    pallas_call x1, Pallas kernels: 76.9 us -> 74.7 us  [potentials(): pl.pallas_call(functools.partial(density_kernel, chips, planes, batches,...]
where the time goes in v5:
time: 112 us; the launch traced here: 110 us
  Pallas kernels  107 us (96%)
  other arithmetic  2.62 us (2%)
    pallas_call x1, Pallas kernels, potentials(): pl.pallas_call(functools.partial(density_kernel, chips, planes, batches,...  74.7 us
    pallas_call x1, Pallas kernels, fock_own(): pl.pallas_call(functools.partial(fock_kernel, batches, share), out_shape=...  27.5 us
    pallas_call x1, Pallas kernels, fock_far(): pl.pallas_call(functools.partial(far_kernel, batches), out_shape=jax.Shap...  5.28 us
    dynamic_update_slice x1, other arithmetic, shards(): lax.dynamic_update_slice(own, present + (arrived * keep)[None], place)  2.43 us
  transfers between devices with their start and end apart: 1, of which 0 were waited for; matrix products, arithmetic and copies ran while one was open for 0% of the time, Pallas kernels for 25%

profile of v5, /device:TPU:9, one launch (start us, length us, event | category | flops | bytes accessed | tf_op | source)
XLA Modules:
  0.0 110.4 jit_solution(11872900335499932633)
XLA Ops:
  0.0 74.7 %potentials.1 = (bf16[6,8,256,768]{3,2,1,0:T(8,128)(2,1)}, s32[8,128]{1,0:T(8,128)}, f32[6,4,2,24,128]{4,3,2,1,0:T(8,128)}, bf16[6,8,2,2,32,128]{5,4,3,2,1,0:T(8,128)(2,1)}, bf16[8,2,32,128]{3,2,1,0:T(8,128)(2,1)}) custom-call(bf16[8,256,768]{2,1,0:T(8,128)(2,1)} %phi_ref.1, bf16[2,12,32,1408]{3,2,1,0:T(8,128)(2,1)} %dens_ref.1, s32[8]{0:T(128)} %starts_ref.1, ...), custom_call_target="tpu_custom_call" | custom-call | flops 16999999488 | bytes 50000000 | tf_op jit(solution)/shard_map/potentials/pallas_call | solution.py:445
  74.7 0.0 copy-start
  74.7 5.3 %fock_far.1 = f32[12,32,768]{2,1,0:T(8,128)} custom-call(s32[8,128]{1,0:T(8,128)} %get-tuple-element.10.facts_ref, f32[48,24,128]{2,1,0:T(8,128)} %bitcast.10, bf16[16,32,128]{2,1,0:T(8,128)(2,1)} %bitcast.12, bf16[6,8,256,768]{3,2,1,0:T(8,128)(2,1)} %get-tuple-element.13.phi_ref), custom_call_target="tpu_custom_call" | custom-call | flops 1000000000 | bytes 2000000 | tf_op jit(solution)/shard_map/fock_far/pallas_call | solution.py:699
  80.0 0.1 collective-permute-start
  80.1 0.0 copy-done
  80.2 0.2 convert_reduce_fusion
  80.3 0.1 broadcast_bitcast_fusion
  80.4 27.5 %fock_own.1 = f32[2,12,32,1408]{3,2,1,0:T(8,128)} custom-call(s32[8,128]{1,0:T(8,128)} %get-tuple-element.10.facts_ref, f32[48,24,128]{2,1,0:T(8,128)} %bitcast.11, bf16[96,2,32,128]{3,2,1,0:T(8,128)(2,1)} %bitcast.14, bf16[6,8,256,768]{3,2,1,0:T(8,128)(2,1)} %get-tuple-element.13.phi_ref), custom_call_target="tpu_custom_call" | custom-call | flops 20000000000 | bytes 20000000 | tf_op jit(solution)/shard_map/fock_own/pallas_call | solution.py:653
  107.9 0.0 collective-permute-done
  107.9 2.4 %fusion = f32[2,12,32,1408]{3,2,1,0:T(8,128)} fusion(f32[2,12,32,1408]{3,2,1,0:T(8,128)} %fock_own.1, s32[]{:T(128)S(6)} %select_n.14, s32[]{:T(128)S(6)} %select_n.15, f32[12,32,768]{2,1,0:T(8,128)S(1)} %collective-permute-done, f32[768]{0:T(1024)S(1)} %broadcast_bitcast_fusion), kind=kLoop, calls=%fused_computation.1 | loop fusion | flops 589824 | bytes 3542024 | tf_op jit(solution)/shard_map/dynamic_update_slice | solution.py:731
Async XLA Ops:
  74.7 5.4 %copy-start = (s32[64,11]{0,1:T(8,128)S(1)}, s32[64,11]{0,1:T(8,128)}, u32[]{:S(2)}) copy-start(s32[64,11]{0,1:T(8,128)} %param.11) | copy-start | bytes 8452
  80.0 27.9 %collective-permute-start = (f32[12,32,768]{2,1,0:T(8,128)}, f32[12,32,768]{2,1,0:T(8,128)S(1)}, u32[]{:S(2)}, u32[]{:S(2)}) collective-permute-start(f32[12,32,768]{2,1,0:T(8,128)} %fock_far.1), channel_id=1, source_target_pairs={{0,124},{4,8},{8,4},{12,16},{16,12},{20,24},{24,20},{28,32},{32,28... | collective-permute-start | bytes 3538952 | tf_op jit(solution)/shard_map/ppermute | solution.py:725

commit v6 on v5

--- a/solution.py
+++ b/solution.py
@@ -486,21 +486,28 @@
     return jnp.concatenate([halves[:PERTS], halves[PERTS:]], axis=1)
 
 
-def split_weights(pot, picked):
+def split_weights(pot, picked, scale):
     weighted = (pot[:, None, :] * picked[None]).reshape(pot.shape[0] * picked.shape[0], picked.shape[1])
     high = weighted.astype(jnp.bfloat16)
-    low = (weighted - high.astype(jnp.float32)).astype(jnp.bfloat16)
+    low = ((weighted - high.astype(jnp.float32)) * scale).astype(EIGHT)
     return high, low
 
 
 CUT = POINTS // 2
 LARGEST = 8
+EIGHT = jnp.float8_e4m3fn
+ROOM = 448.0 / (6.0 * 2.0**-8)
 
 
 class Chunks:
-    def __init__(self, batches, facts_ref, pot, pick, phi_ref, listed, counted, buf, sems):
+    def __init__(self, batches, facts_ref, pot, pick, phi_ref, listed, counted, buf, sems, scale):
         self.batches, self.facts, self.pot, self.pick, self.phi = batches, facts_ref, pot, pick, phi_ref
-        self.listed, self.counted, self.buf, self.sems = listed, counted, buf, sems
+        self.listed, self.counted, self.buf, self.sems, self.scale = listed, counted, buf, sems, scale
+
+    def set_scale(self, pots):
+        most = jnp.maximum(jnp.max(jnp.abs(pots)), 1e-30)
+        self.scale[0] = ROOM / most
+        self.scale[1] = most * (1.0 / ROOM)
 
     def start(self, no):
         return self.facts[no // self.batches, lax.rem(no, self.batches)]
@@ -529,6 +536,7 @@
 
     def group(self, which, at, size, rows):
         rights, highs, lows = [], [[] for _ in rows], [[] for _ in rows]
+        scale = self.scale[0]
         for i in range(size):
             chunk = self.listed[which * self.pot.shape[0] * 2 + at + i]
             self.copy(chunk).wait()
@@ -536,13 +544,15 @@
             pot = jnp.where(lax.rem(chunk, 2) == 0, pots[:PERTS], pots[PERTS:])
             rights.append(self.buf[chunk])
             for no, (row, _) in enumerate(rows):
-                high, low = split_weights(pot, self.pick(chunk, row).astype(jnp.float32))
+                high, low = split_weights(pot, self.pick(chunk, row).astype(jnp.float32), scale)
                 highs[no].append(high)
                 lows[no].append(low)
-        right = jnp.concatenate(rights + rights, axis=0)
-        left = jnp.concatenate(
-            [jnp.concatenate(high + low, axis=1) for high, low in zip(highs, lows)], axis=0)
+        right = jnp.concatenate(rights, axis=0)
+        left = jnp.concatenate([jnp.concatenate(high, axis=1) for high in highs], axis=0)
         total = jnp.dot(left, right, preferred_element_type=jnp.float32)
+        low = jnp.concatenate([jnp.concatenate(low, axis=1) for low in lows], axis=0)
+        rest = jnp.dot(low, right.astype(EIGHT), preferred_element_type=jnp.float32)
+        total = total + rest * self.scale[1]
         depth = left.shape[0] // len(rows)
         for no, (_, spot) in enumerate(rows):
             spot[...] = spot[...] + total[no * depth:(no + 1) * depth].reshape(spot.shape)
@@ -563,13 +573,14 @@
 
 
 def fock_kernel(batches, share, facts_ref, pot_ref, picks_ref, phi_ref, out_ref,
-                total, pot_v, picks_v, listed, counted, buf, sems, in_sem, out_sem):
+                total, pot_v, picks_v, listed, counted, buf, sems, scale, in_sem, out_sem):
     grid_pos = lax.axis_index("grid")
     pot_copy = pltpu.make_async_copy(pot_ref, pot_v, in_sem.at[0])
     pot_copy.start()
     picks_copy = pltpu.make_async_copy(picks_ref, picks_v, in_sem.at[1])
     picks_copy.start()
-    chunks = Chunks(batches, facts_ref, pot_v, lambda chunk, row: picks_v[chunk, row], phi_ref, listed, counted, buf, sems)
+    chunks = Chunks(batches, facts_ref, pot_v, lambda chunk, row: picks_v[chunk, row], phi_ref, listed, counted, buf, sems,
+                    scale)
     base = 2 * grid_pos - REACH
     leads = REACH + 2
 
@@ -585,6 +596,7 @@
     chunks.fetch(1)
     total[...] = jnp.zeros_like(total)
     pot_copy.wait()
+    chunks.set_scale(pot_v[...])
     picks_copy.wait()
 
     def spot(r, offset):
@@ -642,6 +654,7 @@
         pltpu.SMEM((lists,), jnp.int32),
         pltpu.VMEM((most, CUT, cols), dtype),
         pltpu.SemaphoreType.DMA((most,)),
+        pltpu.SMEM((2,), jnp.float32),
     ]
 
 
@@ -666,7 +679,7 @@
     )(facts, pot, picks, phi_all)
 
 
-def far_kernel(batches, facts_ref, pot_ref, picks_ref, phi_ref, out_ref, pot_v, picks_v, listed, counted, buf, sems, in_sem):
+def far_kernel(batches, facts_ref, pot_ref, picks_ref, phi_ref, out_ref, pot_v, picks_v, listed, counted, buf, sems, scale, in_sem):
     grid_pos = lax.axis_index("grid")
     core = lax.rem(grid_pos, 2)
     slot = jnp.where(core == 0, 4, 1)
@@ -677,7 +690,7 @@
     picks_copy = pltpu.make_async_copy(picks_ref, picks_v, in_sem.at[1])
     picks_copy.start()
     chunks = Chunks(batches, facts_ref, pot_v, lambda chunk, row: picks_v[chunk - 2 * batches * slot], phi_ref,
-                    listed, counted, buf, sems)
+                    listed, counted, buf, sems, scale)
     counted[0] = 0
 
     @pl.loop(0, batches)
@@ -687,6 +700,7 @@
     chunks.fetch(0)
     out_ref[...] = jnp.zeros_like(out_ref)
     pot_copy.wait()
+    chunks.set_scale(pot_v[own])
     picks_copy.wait()
     chunks.add(0, [(0, out_ref)])
 

time: 112 us -> 108 us (0.964)
  Pallas kernels: 107 us -> 103 us
    pallas_call x1, Pallas kernels: 27.5 us -> 23.9 us  [fock_own(): pl.pallas_call(functools.partial(fock_kernel, batches, share), out_shape=...]
  transfers between devices with their start and end apart: 1 -> 1, of which waited for: 0 -> 0; matrix products, arithmetic and copies ran while one was open for 0% -> 0% of each run, Pallas kernels for 25% -> 22%
where the time goes in v6:
time: 108 us; the launch traced here: 106 us
  Pallas kernels  103 us (95%)
  other arithmetic  2.62 us (2%)
    pallas_call x1, Pallas kernels, potentials(): pl.pallas_call(functools.partial(density_kernel, chips, planes, batches,...  74.7 us
    pallas_call x1, Pallas kernels, fock_own(): pl.pallas_call(functools.partial(fock_kernel, batches, share), out_shape=...  23.9 us
    pallas_call x1, Pallas kernels, fock_far(): pl.pallas_call(functools.partial(far_kernel, batches), out_shape=jax.Shap...  4.78 us
    dynamic_update_slice x1, other arithmetic, shards(): lax.dynamic_update_slice(own, present + (arrived * keep)[None], place)  2.43 us
  transfers between devices with their start and end apart: 1, of which 0 were waited for; matrix products, arithmetic and copies ran while one was open for 0% of the time, Pallas kernels for 22%

profile of v6, /device:TPU:9, one launch (start us, length us, event | category | flops | bytes accessed | tf_op | source)
XLA Modules:
  0.0 106.2 jit_solution(18207183212318777388)
XLA Ops:
  0.0 74.7 %potentials.1 = (bf16[6,8,256,768]{3,2,1,0:T(8,128)(2,1)}, s32[8,128]{1,0:T(8,128)}, f32[6,4,2,24,128]{4,3,2,1,0:T(8,128)}, bf16[6,8,2,2,32,128]{5,4,3,2,1,0:T(8,128)(2,1)}, bf16[8,2,32,128]{3,2,1,0:T(8,128)(2,1)}) custom-call(bf16[8,256,768]{2,1,0:T(8,128)(2,1)} %phi_ref.1, bf16[2,12,32,1408]{3,2,1,0:T(8,128)(2,1)} %dens_ref.1, s32[8]{0:T(128)} %starts_ref.1, ...), custom_call_target="tpu_custom_call" | custom-call | flops 16999999488 | bytes 50000000 | tf_op jit(solution)/shard_map/potentials/pallas_call | solution.py:445
  74.7 0.0 copy-start
  74.7 4.8 %fock_far.1 = f32[12,32,768]{2,1,0:T(8,128)} custom-call(s32[8,128]{1,0:T(8,128)} %get-tuple-element.10.facts_ref, f32[48,24,128]{2,1,0:T(8,128)} %bitcast.10, bf16[16,32,128]{2,1,0:T(8,128)(2,1)} %bitcast.12, bf16[6,8,256,768]{3,2,1,0:T(8,128)(2,1)} %get-tuple-element.13.phi_ref), custom_call_target="tpu_custom_call" | custom-call | flops 1000000000 | bytes 2000000 | tf_op jit(solution)/shard_map/fock_far/pallas_call | solution.py:713
  79.5 0.1 collective-permute-start
  79.6 0.0 copy-done
  79.7 0.2 convert_reduce_fusion
  79.8 0.1 broadcast_bitcast_fusion
  79.9 23.9 %fock_own.1 = f32[2,12,32,1408]{3,2,1,0:T(8,128)} custom-call(s32[8,128]{1,0:T(8,128)} %get-tuple-element.10.facts_ref, f32[48,24,128]{2,1,0:T(8,128)} %bitcast.11, bf16[96,2,32,128]{3,2,1,0:T(8,128)(2,1)} %bitcast.14, bf16[6,8,256,768]{3,2,1,0:T(8,128)(2,1)} %get-tuple-element.13.phi_ref), custom_call_target="tpu_custom_call" | custom-call | flops 20000000000 | bytes 20000000 | tf_op jit(solution)/shard_map/fock_own/pallas_call | solution.py:666
  103.8 0.0 collective-permute-done
  103.8 2.4 %fusion = f32[2,12,32,1408]{3,2,1,0:T(8,128)} fusion(f32[2,12,32,1408]{3,2,1,0:T(8,128)} %fock_own.1, s32[]{:T(128)S(6)} %select_n.14, s32[]{:T(128)S(6)} %select_n.15, f32[12,32,768]{2,1,0:T(8,128)S(1)} %collective-permute-done, f32[768]{0:T(1024)S(1)} %broadcast_bitcast_fusion), kind=kLoop, calls=%fused_computation.1 | loop fusion | flops 589824 | bytes 3542024 | tf_op jit(solution)/shard_map/dynamic_update_slice | solution.py:745
Async XLA Ops:
  74.7 4.9 %copy-start = (s32[64,11]{0,1:T(8,128)S(1)}, s32[64,11]{0,1:T(8,128)}, u32[]{:S(2)}) copy-start(s32[64,11]{0,1:T(8,128)} %param.11) | copy-start | bytes 8452
  79.5 24.3 %collective-permute-start = (f32[12,32,768]{2,1,0:T(8,128)}, f32[12,32,768]{2,1,0:T(8,128)S(1)}, u32[]{:S(2)}, u32[]{:S(2)}) collective-permute-start(f32[12,32,768]{2,1,0:T(8,128)} %fock_far.1), channel_id=1, source_target_pairs={{0,124},{4,8},{8,4},{12,16},{16,12},{20,24},{24,20},{28,32},{32,28... | collective-permute-start | bytes 3538952 | tf_op jit(solution)/shard_map/ppermute | solution.py:739

commit v7 on v6

--- a/solution.py
+++ b/solution.py
@@ -44,6 +44,12 @@
     there = half - first
     rows_all = PERTS * share
     cut = POINTS // 2
+    has_down, has_up = chip > 0, chip < chips - 1
+    sends, comes = (has_up, has_down), (has_down, has_up)
+    far_exists = jnp.where(core == 0, chip, chips - 1 - chip) > 0
+
+    def exists(d):
+        return jnp.where(d == 0, chip, jnp.where(d == 2, chips - 1 - chip, 1)) > 0
 
     def device(slot, at_plane):
         return (2 * lax.rem(chip + slot // 2 - 1 + chips, chips) + lax.rem(slot, 2), at_plane)
@@ -63,7 +69,7 @@
             turn, at_plane = no // planes, lax.rem(no, planes)
             d = jnp.where(turn == 0, order[0], jnp.where(turn == 1, order[1], order[2]))
 
-            @pl.when(is_other(d, at_plane))
+            @pl.when(jnp.logical_and(is_other(d, at_plane), exists(d)))
             def _():
                 act(d, at_plane)
 
@@ -84,11 +90,15 @@
     meta_all_v[own_slot] = meta
 
     barrier = pltpu.get_barrier_semaphore()
-    for slot in (0, 1, 4, 5):
-        pl.semaphore_signal(barrier, inc=1, device_id=device(slot, plane), device_id_type=MESH)
+    for there_is, slots in ((has_down, (0, 1)), (has_up, (4, 5))):
+        @pl.when(there_is)
+        def _(slots=slots):
+            for slot in slots:
+                pl.semaphore_signal(barrier, inc=1, device_id=device(slot, plane), device_id_type=MESH)
+
     for partner in (other, (grid_pos, lax.rem(plane + 1, planes)), (grid_pos, lax.rem(plane + planes - 1, planes))):
         pl.semaphore_signal(barrier, inc=1, device_id=partner, device_id_type=MESH)
-    pl.semaphore_wait(barrier, 7)
+    pl.semaphore_wait(barrier, 3 + 2 * has_down.astype(jnp.int32) + 2 * has_up.astype(jnp.int32))
 
     def piece(way, n):
         return n // 2 + quarter * lax.rem(n + way, 2)
@@ -128,16 +138,27 @@
 
     core_meta.start()
     for way in range(2):
-        for s in range(2):
-            meta_copy(way, s).start()
+        @pl.when(sends[way])
+        def _(way=way):
+            for s in range(2):
+                meta_copy(way, s).start()
+
+        @pl.when(jnp.logical_not(comes[way]))
+        def _(way=way):
+            for s in range(2):
+                meta_all_v[4 * way + s] = jnp.full((8, BLOCK), -1000, jnp.int32)
 
     @pl.loop(0, half)
     def _(n):
         for h in range(2):
             for way in range(2):
-                y_copy(way, n, h).start()
-
-    far_copy.start()
+                @pl.when(sends[way])
+                def _(way=way, h=h):
+                    y_copy(way, n, h).start()
+
+    @pl.when(far_exists)
+    def _():
+        far_copy.start()
 
     @pl.loop(0, batches)
     def _(no):
@@ -160,8 +181,13 @@
     far_v[rows_all:, :] = one_hot(share, COLS, core * REACH * BLOCK + plane * share)
 
     own_copy.wait()
-    for no in range(5):
-        pltpu.make_async_copy(meta_v, meta_all_v.at[own_slot], m_r.at[no]).wait()
+    pltpu.make_async_copy(meta_v, meta_all_v.at[own_slot], m_r.at[0]).wait()
+    for way in range(2):
+        @pl.when(comes[way])
+        def _(way=way):
+            for s in range(2):
+                pltpu.make_async_copy(meta_v, meta_all_v.at[own_slot], m_r.at[1 + 2 * way + s]).wait()
+
     facts = jnp.zeros((8, BLOCK), jnp.int32)
     for slot in range(SLOTS):
         facts = jnp.where(line == slot, meta_all_v[slot], facts)
@@ -273,14 +299,14 @@
         rho_part(*batch_pair[0], (0, 1))
         rho_part(*batch_pair[1], (1 - core,) if crossed else (0, 1))
         for slot, no in batch_pair:
-            @pl.when(lax.rem(slot, 2) != core)
+            @pl.when(jnp.logical_and(lax.rem(slot, 2) != core, exists(slot // 2)))
             def _():
                 mate_copy(slot // 2, no).start()
 
     def combine_pair(m):
         late = jnp.where(lax.rem(m, 2) == 0, 1, 0)
         for slot, no in pair((m - 3 - late) // 2, False, late == 1):
-            @pl.when(slot != far_slot)
+            @pl.when(jnp.logical_and(slot != far_slot, exists(slot // 2)))
             def _():
                 combine(slot // 2, no)
 
@@ -292,9 +318,11 @@
         def _():
             n, h = m // 2, lax.rem(m, 2)
             for way in range(2):
-                y_copy(way, n, h).wait_recv()
-                z_copy(way, n, h).start()
-                c_copy(way, n, h).start()
+                @pl.when(comes[way])
+                def _(way=way):
+                    y_copy(way, n, h).wait_recv()
+                    z_copy(way, n, h).start()
+                    c_copy(way, n, h).start()
 
         @pl.when(jnp.logical_or(m == 1, m == 2))
         def _():
@@ -305,8 +333,10 @@
         def _():
             late = lax.rem(m, 2)
             for way in range(2):
-                for h in range(2):
-                    c_copy(way, late * half + (m - 2 - late) // 2, h).wait_recv()
+                @pl.when(comes[way])
+                def _(way=way):
+                    for h in range(2):
+                        c_copy(way, late * half + (m - 2 - late) // 2, h).wait_recv()
 
         @pl.when(m == half + 1)
         def _():
@@ -324,8 +354,10 @@
         def _():
             n, h = (m - 1) // 2, lax.rem(m - 1, 2)
             for way in range(2):
-                z_copy(way, n, h).wait_recv()
-                c_copy(way, half + n, h).start()
+                @pl.when(comes[way])
+                def _(way=way):
+                    z_copy(way, n, h).wait_recv()
+                    c_copy(way, half + n, h).start()
 
         items_after(m, compute)
 
@@ -334,18 +366,25 @@
             combine_pair(m)
 
     combine_pair(2 * half + 2)
-    far_copy.wait_recv()
-    far_row = jnp.where(core == 0, jnp.maximum(2 * grid_pos - 1, 0), jnp.minimum(2 * grid_pos + 2, 4 * chips - 1))
-    for t in range(WINDOW):
-        block = left_far[:, :, t * BLOCK:(t + 1) * BLOCK].reshape(rows_all, BLOCK)
-        keep = mask_s[jnp.where(core == 0, REACH, 0) + t, far_row]
-        far_v[:rows_all, t * BLOCK:(t + 1) * BLOCK] = masked(block, keep)
+    @pl.when(far_exists)
+    def _():
+        far_copy.wait_recv()
+        far_row = jnp.where(core == 0, jnp.maximum(2 * grid_pos - 1, 0), jnp.minimum(2 * grid_pos + 2, 4 * chips - 1))
+        for t in range(WINDOW):
+            block = left_far[:, :, t * BLOCK:(t + 1) * BLOCK].reshape(rows_all, BLOCK)
+            keep = mask_s[jnp.where(core == 0, REACH, 0) + t, far_row]
+            far_v[:rows_all, t * BLOCK:(t + 1) * BLOCK] = masked(block, keep)
 
     @pl.loop(0, half)
     def _(two):
-        rho_far(two)
-        for i in range(2):
-            combine(far_slot // 2, 2 * two + i)
+        @pl.when(far_exists)
+        def _():
+            rho_far(two)
+
+        @pl.when(exists(far_slot // 2))
+        def _():
+            for i in range(2):
+                combine(far_slot // 2, 2 * two + i)
 
     picks_out = pltpu.make_async_copy(picks_v, picks_ref, own_sem.at[1])
     picks_out.start()
@@ -365,6 +404,16 @@
     def wait_parts(d, at_plane):
         for which in range(per_plane):
             pltpu.make_async_copy(part.at[0, 0], gathered.at[d, at_plane, which], a_r.at[d, at_plane, which]).wait()
+
+    def no_pot_copy(way, s):
+        return pltpu.make_async_copy(gathered.at[2 * way], pot_ref.at[4 * way + s], own_sem.at[5 + 2 * way + s])
+
+    for way in range(2):
+        @pl.when(jnp.logical_not(comes[way]))
+        def _(way=way):
+            gathered[2 * way] = jnp.zeros((planes, per_plane, 2 * PERTS, cut), jnp.float32)
+            for s in range(2):
+                no_pot_copy(way, s).start()
 
     for_others(wait_parts)
     points = lax.broadcasted_iota(jnp.int32, (1, POINTS), 1)
@@ -386,11 +435,22 @@
     facts_out.wait()
     picks_out.wait()
     far_picks_out.wait()
-    far_copy.wait_send()
+
+    @pl.when(far_exists)
+    def _():
+        far_copy.wait_send()
+
     core_meta.wait_send()
     for way in range(2):
-        for s in range(2):
-            meta_copy(way, s).wait_send()
+        @pl.when(sends[way])
+        def _(way=way):
+            for s in range(2):
+                meta_copy(way, s).wait_send()
+
+        @pl.when(jnp.logical_not(comes[way]))
+        def _(way=way):
+            for s in range(2):
+                no_pot_copy(way, s).wait()
 
     @pl.loop(0, batches)
     def _(no):
@@ -398,20 +458,27 @@
         for slot in range(SLOTS):
             out_copy(slot, no).wait()
         for d in range(3):
-            mate_copy(d, no).wait_send()
-
-            @pl.when(is_other(d, no // per_plane))
-            def _():
+            @pl.when(exists(d))
+            def _(d=d):
+                mate_copy(d, no).wait_send()
+
+            @pl.when(jnp.logical_and(is_other(d, no // per_plane), exists(d)))
+            def _(d=d):
                 part_copy(d, no).wait_send()
 
     @pl.loop(0, half)
     def _(n):
         for h in range(2):
             for way in range(2):
-                y_copy(way, n, h).wait_send()
-                z_copy(way, n, h).wait_send()
-                c_copy(way, n, h).wait_send()
-                c_copy(way, half + n, h).wait_send()
+                @pl.when(sends[way])
+                def _(way=way, h=h):
+                    y_copy(way, n, h).wait_send()
+
+                @pl.when(comes[way])
+                def _(way=way, h=h):
+                    z_copy(way, n, h).wait_send()
+                    c_copy(way, n, h).wait_send()
+                    c_copy(way, half + n, h).wait_send()
 
     def pass_on(d, at_plane):
         pltpu.make_async_copy(pot_v, pot_ref.at[2 * d + core, at_plane], b_r.at[d, at_plane]).wait()
@@ -421,7 +488,9 @@
 
     @pl.loop(0, 3 * planes)
     def _(no):
-        cross_copy(no // planes, lax.rem(no, planes)).wait_recv()
+        @pl.when(exists(no // planes))
+        def _():
+            cross_copy(no // planes, lax.rem(no, planes)).wait_recv()
 
     pot_own.wait()
     own_cross.wait_send()
@@ -470,7 +539,7 @@
             pltpu.VMEM((3, batches) + row_pair, f32),
             pltpu.VMEM((3, planes, per_plane) + row_pair, f32),
             pltpu.VMEM((per_plane,) + row_pair, f32),
-            dma((5,)), dma((SLOTS, batches)), dma((batches,)), dma((batches,)),
+            dma((9,)), dma((SLOTS, batches)), dma((batches,)), dma((batches,)),
             dma((2, half, 2)), dma((2, half, 2)), dma((2, half, 2)), dma((2, half, 2)),
             dma((2, batches, 2)), dma((2, batches, 2)), dma((5,)), dma((5,)), dma((2,)),
             dma((3, batches)), dma((3, batches)), dma((3, batches)), dma((3, planes, per_plane)),
@@ -735,7 +804,7 @@
     picks = picks.reshape(2 * SLOTS * batches, 2, share, POINTS // 2)
     far_picks = far_picks.reshape(2 * batches, share, POINTS // 2)
     far = fock_far(facts, pot, far_picks, phi_all, share)
-    route = [(i, (i + 1) % grid_size if i % 2 else (i - 1) % grid_size) for i in range(grid_size)]
+    route = [(i, i + 1 if i % 2 else i - 1) for i in range(1, grid_size - 1)]
     arrived = lax.ppermute(far, "grid", route)
     own = fock_own(facts, pot, picks, phi_all, share)
     mask_row = lax.dynamic_slice(pair_mask, (2 * grid_pos + core, core * REACH), (1, WINDOW))[0]

time: 108 us -> 106 us (0.981)
  Pallas kernels: 103 us -> 98 us
  starting transfers between devices: 0.08 us -> 3.27 us
    pallas_call x1, Pallas kernels: 74.7 us -> 68.6 us  [potentials(): pl.pallas_call(functools.partial(density_kernel, chips, planes, batches,...]
    ppermute x1, starting transfers between devices: 0.08 us -> 3.27 us  [shards(): arrived = lax.ppermute(far, 'grid', route)]
  transfers between devices with their start and end apart: 1 -> 1, of which waited for: 0 -> 0; matrix products, arithmetic and copies ran while one was open for 0% -> 0% of each run, Pallas kernels for 22% -> 24%
where the time goes in v7:
time: 106 us; the launch traced here: 104 us
  Pallas kernels  98 us (92%)
  starting transfers between devices  3.27 us (3%)
  other arithmetic  2.62 us (2%)
    pallas_call x1, Pallas kernels, potentials(): pl.pallas_call(functools.partial(density_kernel, chips, planes, batches,...  68.6 us
    pallas_call x1, Pallas kernels, fock_own(): pl.pallas_call(functools.partial(fock_kernel, batches, share), out_shape=...  24.7 us
    pallas_call x1, Pallas kernels, fock_far(): pl.pallas_call(functools.partial(far_kernel, batches), out_shape=jax.Shap...  4.76 us
    ppermute x1, starting transfers between devices, shards(): arrived = lax.ppermute(far, 'grid', route)  3.27 us
    dynamic_update_slice x1, other arithmetic, shards(): lax.dynamic_update_slice(own, present + (arrived * keep)[None], place)  2.43 us
  transfers between devices with their start and end apart: 1, of which 0 were waited for; matrix products, arithmetic and copies ran while one was open for 0% of the time, Pallas kernels for 24%

profile of v7, /device:TPU:9, one launch (start us, length us, event | category | flops | bytes accessed | tf_op | source)
XLA Modules:
  0.0 104.1 jit_solution(12501388876467700448)
XLA Ops:
  0.0 68.6 %potentials.1 = (bf16[6,8,256,768]{3,2,1,0:T(8,128)(2,1)}, s32[8,128]{1,0:T(8,128)}, f32[6,4,2,24,128]{4,3,2,1,0:T(8,128)}, bf16[6,8,2,2,32,128]{5,4,3,2,1,0:T(8,128)(2,1)}, bf16[8,2,32,128]{3,2,1,0:T(8,128)(2,1)}) custom-call(bf16[8,256,768]{2,1,0:T(8,128)(2,1)} %phi_ref.1, bf16[2,12,32,1408]{3,2,1,0:T(8,128)(2,1)} %dens_ref.1, s32[8]{0:T(128)} %starts_ref.1, ...), custom_call_target="tpu_custom_call" | custom-call | flops 16999999488 | bytes 50000000 | tf_op jit(solution)/shard_map/potentials/pallas_call | solution.py:514
  68.6 0.0 copy-start
  68.6 4.8 %fock_far.1 = f32[12,32,768]{2,1,0:T(8,128)} custom-call(s32[8,128]{1,0:T(8,128)} %get-tuple-element.10.facts_ref, f32[48,24,128]{2,1,0:T(8,128)} %bitcast.10, bf16[16,32,128]{2,1,0:T(8,128)(2,1)} %bitcast.12, bf16[6,8,256,768]{3,2,1,0:T(8,128)(2,1)} %get-tuple-element.13.phi_ref), custom_call_target="tpu_custom_call" | custom-call | flops 1000000000 | bytes 2000000 | tf_op jit(solution)/shard_map/fock_far/pallas_call | solution.py:782
  73.3 3.3 %collective-permute-start = (f32[12,32,768]{2,1,0:T(8,128)}, f32[12,32,768]{2,1,0:T(8,128)S(1)}, u32[]{:S(2)}, u32[]{:S(2)}) collective-permute-start(f32[12,32,768]{2,1,0:T(8,128)} %fock_far.1), channel_id=1, source_target_pairs={{4,8},{8,4},{12,16},{16,12},{20,24},{24,20},{28,32},{32,28},{36,40... | collective-permute-start | bytes 3538952 | tf_op jit(solution)/shard_map/ppermute | solution.py:808
  76.6 0.0 copy-done
  76.6 0.2 convert_reduce_fusion
  76.8 0.1 broadcast_bitcast_fusion
  76.9 24.7 %fock_own.1 = f32[2,12,32,1408]{3,2,1,0:T(8,128)} custom-call(s32[8,128]{1,0:T(8,128)} %get-tuple-element.10.facts_ref, f32[48,24,128]{2,1,0:T(8,128)} %bitcast.11, bf16[96,2,32,128]{3,2,1,0:T(8,128)(2,1)} %bitcast.14, bf16[6,8,256,768]{3,2,1,0:T(8,128)(2,1)} %get-tuple-element.13.phi_ref), custom_call_target="tpu_custom_call" | custom-call | flops 20000000000 | bytes 20000000 | tf_op jit(solution)/shard_map/fock_own/pallas_call | solution.py:735
  101.6 0.0 collective-permute-done
  101.6 2.4 %fusion = f32[2,12,32,1408]{3,2,1,0:T(8,128)} fusion(f32[2,12,32,1408]{3,2,1,0:T(8,128)} %fock_own.1, s32[]{:T(128)S(6)} %select_n.14, s32[]{:T(128)S(6)} %select_n.15, f32[12,32,768]{2,1,0:T(8,128)S(1)} %collective-permute-done, f32[768]{0:T(1024)S(1)} %broadcast_bitcast_fusion), kind=kLoop, calls=%fused_computation.1 | loop fusion | flops 589824 | bytes 3542024 | tf_op jit(solution)/shard_map/dynamic_update_slice | solution.py:814
Async XLA Ops:
  68.6 8.1 %copy-start = (s32[64,11]{0,1:T(8,128)S(1)}, s32[64,11]{0,1:T(8,128)}, u32[]{:S(2)}) copy-start(s32[64,11]{0,1:T(8,128)} %param.11) | copy-start | bytes 8452
  73.3 28.3 %collective-permute-start = (f32[12,32,768]{2,1,0:T(8,128)}, f32[12,32,768]{2,1,0:T(8,128)S(1)}, u32[]{:S(2)}, u32[]{:S(2)}) collective-permute-start(f32[12,32,768]{2,1,0:T(8,128)} %fock_far.1), channel_id=1, source_target_pairs={{4,8},{8,4},{12,16},{16,12},{20,24},{24,20},{28,32},{32,28},{36,40... | collective-permute-start | bytes 3538952 | tf_op jit(solution)/shard_map/ppermute | solution.py:808

commit v8 on v7

--- a/solution.py
+++ b/solution.py
@@ -804,7 +804,7 @@
     picks = picks.reshape(2 * SLOTS * batches, 2, share, POINTS // 2)
     far_picks = far_picks.reshape(2 * batches, share, POINTS // 2)
     far = fock_far(facts, pot, far_picks, phi_all, share)
-    route = [(i, i + 1 if i % 2 else i - 1) for i in range(1, grid_size - 1)]
+    route = [(i, (i + 1) % grid_size if i % 2 else (i - 1) % grid_size) for i in range(grid_size)]
     arrived = lax.ppermute(far, "grid", route)
     own = fock_own(facts, pot, picks, phi_all, share)
     mask_row = lax.dynamic_slice(pair_mask, (2 * grid_pos + core, core * REACH), (1, WINDOW))[0]

time: 106 us -> 104 us (0.981)
  the two profiles are of different devices: /device:TPU:9 before, /device:TPU:6 now
where the time goes in v8:
time: 104 us; the launch traced here: 102 us
  Pallas kernels  95.4 us (92%)
  starting transfers between devices  4.13 us (4%)
  other arithmetic  2.62 us (3%)
    pallas_call x1, Pallas kernels, potentials(): pl.pallas_call(functools.partial(density_kernel, chips, planes, batches,...  71.1 us
    pallas_call x1, Pallas kernels, fock_own(): pl.pallas_call(functools.partial(fock_kernel, batches, share), out_shape=...  20 us
    pallas_call x1, Pallas kernels, fock_far(): pl.pallas_call(functools.partial(far_kernel, batches), out_shape=jax.Shap...  4.37 us
    ppermute x1, starting transfers between devices, shards(): arrived = lax.ppermute(far, 'grid', route)  4.13 us
    dynamic_update_slice x1, other arithmetic, shards(): lax.dynamic_update_slice(own, present + (arrived * keep)[None], place)  2.43 us
  transfers between devices with their start and end apart: 1, of which 0 were waited for; matrix products, arithmetic and copies ran while one was open for 0% of the time, Pallas kernels for 20%

profile of v8, /device:TPU:6, one launch (start us, length us, event | category | flops | bytes accessed | tf_op | source)
XLA Modules:
  0.0 102.3 jit_solution(14127891915968510895)
XLA Ops:
  0.0 71.1 %potentials.1 = (bf16[6,8,256,768]{3,2,1,0:T(8,128)(2,1)}, s32[8,128]{1,0:T(8,128)}, f32[6,4,2,24,128]{4,3,2,1,0:T(8,128)}, bf16[6,8,2,2,32,128]{5,4,3,2,1,0:T(8,128)(2,1)}, bf16[8,2,32,128]{3,2,1,0:T(8,128)(2,1)}) custom-call(bf16[8,256,768]{2,1,0:T(8,128)(2,1)} %phi_ref.1, bf16[2,12,32,1408]{3,2,1,0:T(8,128)(2,1)} %dens_ref.1, s32[8]{0:T(128)} %starts_ref.1, ...), custom_call_target="tpu_custom_call" | custom-call | flops 16999999488 | bytes 50000000 | tf_op jit(solution)/shard_map/potentials/pallas_call | solution.py:514
  71.1 0.0 copy-start
  71.1 4.4 %fock_far.1 = f32[12,32,768]{2,1,0:T(8,128)} custom-call(s32[8,128]{1,0:T(8,128)} %get-tuple-element.10.facts_ref, f32[48,24,128]{2,1,0:T(8,128)} %bitcast.10, bf16[16,32,128]{2,1,0:T(8,128)(2,1)} %bitcast.12, bf16[6,8,256,768]{3,2,1,0:T(8,128)(2,1)} %get-tuple-element.13.phi_ref), custom_call_target="tpu_custom_call" | custom-call | flops 1000000000 | bytes 2000000 | tf_op jit(solution)/shard_map/fock_far/pallas_call | solution.py:782
  75.5 4.1 %collective-permute-start = (f32[12,32,768]{2,1,0:T(8,128)}, f32[12,32,768]{2,1,0:T(8,128)S(1)}, u32[]{:S(2)}, u32[]{:S(2)}) collective-permute-start(f32[12,32,768]{2,1,0:T(8,128)} %fock_far.1), channel_id=1, source_target_pairs={{0,124},{4,8},{8,4},{12,16},{16,12},{20,24},{24,20},{28,32},{32,28... | collective-permute-start | bytes 3538952 | tf_op jit(solution)/shard_map/ppermute | solution.py:808
  79.6 0.0 copy-done
  79.6 0.2 convert_reduce_fusion
  79.8 0.1 broadcast_bitcast_fusion
  79.9 20.0 %fock_own.1 = f32[2,12,32,1408]{3,2,1,0:T(8,128)} custom-call(s32[8,128]{1,0:T(8,128)} %get-tuple-element.10.facts_ref, f32[48,24,128]{2,1,0:T(8,128)} %bitcast.11, bf16[96,2,32,128]{3,2,1,0:T(8,128)(2,1)} %bitcast.14, bf16[6,8,256,768]{3,2,1,0:T(8,128)(2,1)} %get-tuple-element.13.phi_ref), custom_call_target="tpu_custom_call" | custom-call | flops 20000000000 | bytes 20000000 | tf_op jit(solution)/shard_map/fock_own/pallas_call | solution.py:735
  99.9 0.0 collective-permute-done
  99.9 2.4 %fusion = f32[2,12,32,1408]{3,2,1,0:T(8,128)} fusion(f32[2,12,32,1408]{3,2,1,0:T(8,128)} %fock_own.1, s32[]{:T(128)S(6)} %select_n.14, s32[]{:T(128)S(6)} %select_n.15, f32[12,32,768]{2,1,0:T(8,128)S(1)} %collective-permute-done, f32[768]{0:T(1024)S(1)} %broadcast_bitcast_fusion), kind=kLoop, calls=%fused_computation.1 | loop fusion | flops 589824 | bytes 3542024 | tf_op jit(solution)/shard_map/dynamic_update_slice | solution.py:814
Async XLA Ops:
  71.1 8.5 %copy-start = (s32[64,11]{0,1:T(8,128)S(1)}, s32[64,11]{0,1:T(8,128)}, u32[]{:S(2)}) copy-start(s32[64,11]{0,1:T(8,128)} %param.11) | copy-start | bytes 8452
  75.5 24.4 %collective-permute-start = (f32[12,32,768]{2,1,0:T(8,128)}, f32[12,32,768]{2,1,0:T(8,128)S(1)}, u32[]{:S(2)}, u32[]{:S(2)}) collective-permute-start(f32[12,32,768]{2,1,0:T(8,128)} %fock_far.1), channel_id=1, source_target_pairs={{0,124},{4,8},{8,4},{12,16},{16,12},{20,24},{24,20},{28,32},{32,28... | collective-permute-start | bytes 3538952 | tf_op jit(solution)/shard_map/ppermute | solution.py:808
